TPU v7x, 128 devices: a whole 4x4x4 slice. The times are simulated.
128 devices in a mesh: dp: 8 (over y, core), seq: 16 (over x, z).
Axes of the slice: x: 4, y: 4, z: 4, core: 2. Of those that a mesh axis runs over, the one named last changes fastest.
Arguments:
- queries: bfloat16 [8, 6144, 2048], P('dp', 'seq'), may hold values from -256 to 256
- database: bfloat16 [64, 128, 896], P('seq'), may hold values from -6 to 6
- kv_weight: bfloat16 [896, 4096], replicated, may hold values from -1 to 1
- neighbours: int32 [8, 96, 2], P('dp', 'seq'), may hold values from 0 to 63, as said below
- out_grad: bfloat16 [8, 6144, 2048], P('dp', 'seq'), may hold values from -12 to 12
Outputs:
- attended: bfloat16 [8, 6144, 2048], P('dp', 'seq')
- query_grad: bfloat16 [8, 6144, 2048], P('dp', 'seq')
- row_grad: float32 [64, 128, 896], P('seq', 'dp')
Inputs may be any that keep to these rules, and one draw needn't show every extreme that they name: `neighbours`: neighbour n is held by index n // 4 of seq. The two ids of a group differ. Among the ids of groups s * 6 - 1 to s * 6 + 4 of one sequence (groups from 0 on), at most 2 are held by one index of seq, and in each such set at least one index is named exactly 2 times; in one of the sequences such an index is the same for every s.
All inputs are finite; a program needn't handle non-finite values.
Results may differ from a plain program's by a relative error of at most 0.02.
The roundings to bfloat16 on the way count: a program that leaves them out, or rounds other values in their place, can miss the bound.
Values may be sent and summed in bfloat16 or wider, within the bound.
No kernel may reach another device: no remote copies, remote signals or barrier semaphores. Data moves between devices by JAX's collectives and lax.ppermute only.
A program may use at most 192 MiB of HBM per device.

v0:
```python
import functools

import jax
import jax.numpy as jnp
from jax import lax
from jax.experimental import pallas as pl
from jax.experimental.pallas import tpu as pltpu
from jax.sharding import Mesh
from jax.sharding import PartitionSpec as P

HD = 128
GROUP = 64
SEQ = ("x", "z")
DP = ("y", "c")
LINE = ("y", "c", "x")
CHUNKS = 2
HEAD_BATCH = 8
F32 = jnp.float32
BF16 = jnp.bfloat16


def dot(a, b, ca, cb):
    return lax.dot_general(a, b, (((ca,), (cb,)), ((), ())), preferred_element_type=F32)


def pack_kernel(first_group, group_count, chunk_groups, ids_ref, table_ref, out_ref):
    def per_dest(dest, carry):
        for g in range(chunk_groups):
            at = dest * 2 * group_count + 2 * (first_group + g)
            first, second = ids_ref[at], ids_ref[at + 1]
            a = table_ref[first >> 2, first & 3].astype(F32)
            b = table_ref[second >> 2, second & 3].astype(F32)
            out_ref[dest, g] = jnp.concatenate([a[:4], b[:4], a[4:], b[4:]], axis=0).astype(BF16)
        return carry

    lax.fori_loop(0, out_ref.shape[0], per_dest, 0)


def pack(ids, table, first_group, group_count, chunk_groups):
    dests, enc = table.shape[0], table.shape[-1]
    return pl.pallas_call(
        functools.partial(pack_kernel, first_group, group_count, chunk_groups),
        out_shape=jax.ShapeDtypeStruct((dests, chunk_groups, 16, enc), BF16),
        in_specs=[
            pl.BlockSpec(memory_space=pltpu.SMEM),
            pl.BlockSpec(memory_space=pltpu.VMEM),
        ],
        out_specs=pl.BlockSpec(memory_space=pltpu.VMEM),
        compiler_params=pltpu.CompilerParams(vmem_limit_bytes=16 << 20),
        name="pack",
    )(ids, table)


def attend_kernel(
    heads, first_group, live_ref, rows_ref, w_ref, q_ref, g_ref, *rest
):
    att_ref, qg_ref, term_ref, kv, kv_grad, q_turned, g_turned = rest[-7:]
    scale = HD**-0.5
    width = heads * HD
    live = (live_ref[0] > 0) | (pl.program_id(0) + first_group > 0)
    rows = rows_ref[...].reshape(-1, rows_ref.shape[-1])
    kv[...] = dot(rows, w_ref[...], 1, 0).astype(BF16)
    grads = jnp.where(live, g_ref[...], jnp.zeros((), BF16))
    q_turned[...] = jnp.transpose(q_ref[...])
    g_turned[...] = jnp.transpose(grads)
    for base in range(0, heads, HEAD_BATCH):
        keys = [slice(h * HD, (h + 1) * HD) for h in range(base, base + HEAD_BATCH)]
        values = [slice(width + h * HD, width + (h + 1) * HD) for h in range(base, base + HEAD_BATCH)]
        scores = [dot(q_ref[:, k], kv[:, k], 1, 1) * scale for k in keys]
        grad_probs = [dot(grads[:, k], kv[:, v], 1, 1) for k, v in zip(keys, values)]
        raised = [jnp.exp(s - jnp.max(s, axis=-1, keepdims=True)) for s in scores]
        probs = [e / jnp.sum(e, axis=-1, keepdims=True) for e in raised]
        halves = [p.astype(BF16) for p in probs]
        score_grads = [
            (p * (gp - jnp.sum(p * gp, axis=-1, keepdims=True))).astype(BF16)
            for p, gp in zip(probs, grad_probs)
        ]
        for k, v, half, sg in zip(keys, values, halves, score_grads):
            att_ref[:, k] = jnp.where(live, dot(half, kv[:, v], 1, 0), 0.0).astype(BF16)
            qg_ref[:, k] = (dot(sg, kv[:, k], 1, 0) * scale).astype(BF16)
            kv_grad[k, :] = (dot(q_turned[k, :], sg, 1, 0) * scale).astype(BF16)
            kv_grad[v, :] = dot(g_turned[k, :], half, 1, 0).astype(BF16)
    terms = jnp.transpose(dot(w_ref[...], kv_grad[...], 1, 0)).astype(BF16)
    term_ref[...] = terms.reshape(term_ref.shape)


def attend(live, rows, weight, queries, grads, before, first_group, line):
    slices, chunk_groups, _, enc = rows.shape
    tokens, width = queries.shape
    keys = slices * 16
    block = pl.BlockSpec((GROUP, width), lambda i, l: (i + first_group, 0))
    flops = chunk_groups * (2 * 2 * keys * enc * 2 * width + 6 * 2 * GROUP * keys * width)
    return pl.pallas_call(
        functools.partial(attend_kernel, width // HD, first_group),
        out_shape=[
            jax.ShapeDtypeStruct((tokens, width), BF16),
            jax.ShapeDtypeStruct((tokens, width), BF16),
            jax.ShapeDtypeStruct((line, chunk_groups, keys // line, enc), BF16),
        ],
        grid_spec=pltpu.PrefetchScalarGridSpec(
            num_scalar_prefetch=1,
            grid=(chunk_groups,),
            in_specs=[
                pl.BlockSpec((slices, 1, 16, enc), lambda i, l: (0, i, 0, 0)),
                pl.BlockSpec((enc, 2 * width), lambda i, l: (0, 0)),
                block,
                block,
            ]
            + [pl.BlockSpec(memory_space=pl.ANY)] * len(before),
            out_specs=[
                block,
                block,
                pl.BlockSpec((line, 1, keys // line, enc), lambda i, l: (0, i, 0, 0)),
            ],
            scratch_shapes=[
                pltpu.VMEM((keys, 2 * width), BF16),
                pltpu.VMEM((2 * width, keys), BF16),
                pltpu.VMEM((width, GROUP), BF16),
                pltpu.VMEM((width, GROUP), BF16),
            ],
        ),
        input_output_aliases={5 + n: n for n in range(len(before))},
        cost_estimate=pl.CostEstimate(
            flops=flops, bytes_accessed=16 << 20, transcendentals=0
        ),
        compiler_params=pltpu.CompilerParams(vmem_limit_bytes=44 << 20),
        name="attend",
    )(live, rows, weight, queries, grads, *before)


def exchange(block, axes):
    return lax.all_to_all(block, axes, split_axis=0, concat_axis=0, tiled=True)


def body(queries, database, kv_weight, neighbours, out_grad):
    seq_count = lax.axis_size(SEQ)
    seq_index = lax.axis_index(SEQ)
    x_count, z_count = lax.axis_size("x"), lax.axis_size("z")
    dp_count = lax.axis_size(DP)
    line = lax.axis_size(LINE)
    group_count = neighbours.shape[1]
    ref_count = 2 * group_count
    held, row_tokens, enc = database.shape
    width = queries.shape[2]
    chunk_groups = group_count // CHUNKS
    own_tokens = row_tokens // line

    slices = database.reshape(held, seq_count, row_tokens // seq_count, enc).transpose(1, 0, 2, 3)
    id_rows = jnp.pad(
        neighbours.reshape(1, ref_count).astype(BF16), ((0, row_tokens // seq_count - 1), (0, enc - ref_count))
    )
    id_rows = jnp.broadcast_to(id_rows[None, None], (seq_count, 1) + id_rows.shape)
    table = exchange(jnp.concatenate([slices, id_rows], axis=1), SEQ)
    all_ids = table[:, held, 0, :ref_count].astype(jnp.int32).reshape(-1)
    windows = jnp.concatenate([all_ids[:2], all_ids[:-2]])

    live = (seq_index > 0).astype(jnp.int32).reshape(1)
    rows = [
        exchange(pack(windows, table, c * chunk_groups, group_count, chunk_groups), SEQ)
        for c in range(CHUNKS)
    ]

    z_index = lax.axis_index("z")
    column = lax.dynamic_index_in_dim(
        windows.reshape(x_count, z_count, ref_count), z_index, axis=1, keepdims=False
    )
    column_live = (
        (jnp.arange(x_count)[:, None] > 0) | (z_index > 0) | (jnp.arange(ref_count)[None, :] >= 2)
    )
    column = jnp.where(column_live, column, -1)
    line_ids = lax.all_gather(column, DP, axis=0, tiled=False).reshape(line, group_count, 2)
    keys = jnp.where(
        line_ids[..., None] >= 0, line_ids[..., None] * own_tokens + jnp.arange(own_tokens), -1
    )

    done = ()
    total = jnp.zeros((seq_count * held * own_tokens, enc), F32)
    for c in range(CHUNKS):
        *done, terms = attend(
            live, rows[c], kv_weight, queries[0], out_grad[0], done, c * chunk_groups, line
        )
        back = exchange(terms, LINE)
        chunk_keys = keys[:, c * chunk_groups : (c + 1) * chunk_groups].reshape(1, -1)
        match = (jnp.arange(total.shape[0])[:, None] == chunk_keys).astype(BF16)
        total = total + jnp.dot(match, back.reshape(-1, enc), preferred_element_type=F32)
    owned = exchange(total.astype(BF16).reshape(seq_count, held * own_tokens, enc), SEQ)
    owned = owned.reshape(x_count, z_count, held, own_tokens, enc).astype(F32).sum(axis=1)
    row_grad = owned.transpose(1, 0, 2, 3).reshape(held, x_count * own_tokens, enc)
    return done[0][None], done[1][None], row_grad


def solution(mesh):
    split = Mesh(mesh.devices.reshape(4, 2, 4, 4), ("y", "c", "x", "z"))
    return jax.shard_map(
        body,
        mesh=split,
        in_specs=(
            P(DP, SEQ, None),
            P(SEQ, None, None),
            P(),
            P(DP, SEQ, None),
            P(DP, SEQ, None),
        ),
        out_specs=(P(DP, SEQ, None), P(DP, SEQ, None), P(SEQ, DP, None)),
        check_vma=False,
    )
```

profile of v0, /device:TPU:0, one launch (start us, length us, event | category | flops | bytes accessed | tf_op | source)
XLA Modules:
  0.0 177.7 jit_solution(7448284088436712735)
XLA Ops:
  0.7 1.2 copy-done
  2.3 25.9 %all_to_all.30.table_ref = bf16[16,5,8,896]{3,2,1,0:T(8,128)(2,1)S(1)} all-to-all(bf16[16,5,8,896]{3,2,1,0:T(8,128)(2,1)S(1)} %pad_maximum_fusion), channel_id=1, replica_groups=mesh['y'=4,'c'=2,'x'=4,'z'=4] {'x','z'}, dimensions={0} | all-to-all | bytes 2293760 | tf_op jit(solution)/shard_map/all_to_all | solution.py:132
  28.4 2.1 %pack.3 = bf16[16,3,16,896]{3,2,1,0:T(8,128)(2,1)} custom-call(s32[192]{0:T(256)S(1)} %pad_add_fusion.ids_ref, bf16[16,5,8,896]{3,2,1,0:T(8,128)(2,1)S(1)} %all_to_all.30.table_ref), custom_call_target="tpu_custom_call" | custom-call | tf_op jit(solution)/shard_map/pack/pallas_call | solution.py:41
  30.5 3.7 %all-to-all-start.2 = ((bf16[16,3,16,896]{3,2,1,0:T(8,128)(2,1)}), bf16[16,3,16,896]{3,2,1,0:T(8,128)(2,1)S(1)}, u32[]{:S(2)}, u32[]{:S(2)}) async-start(bf16[16,3,16,896]{3,2,1,0:T(8,128)(2,1)} %pack.3), calls=%async_computation.2 | async-start | bytes 2752512 | tf_op jit(solution)/shard_map/all_to_all | solution.py:132
  34.3 2.1 %pack.2 = bf16[16,3,16,896]{3,2,1,0:T(8,128)(2,1)} custom-call(s32[192]{0:T(256)S(1)} %pad_add_fusion.ids_ref, bf16[16,5,8,896]{3,2,1,0:T(8,128)(2,1)S(1)} %all_to_all.30.table_ref), custom_call_target="tpu_custom_call" | custom-call | tf_op jit(solution)/shard_map/pack/pallas_call | solution.py:41
  36.4 18.0 %all-to-all-done.2.rows_ref = bf16[16,3,16,896]{3,2,1,0:T(8,128)(2,1)S(1)} async-done(((bf16[16,3,16,896]{3,2,1,0:T(8,128)(2,1)}), bf16[16,3,16,896]{3,2,1,0:T(8,128)(2,1)S(1)}, u32[]{:S(2)}, u32[]{:S(2)}) %all-to-all-start.2) | async-done | bytes 1376288 | tf_op jit(solution)/shard_map/all_to_all | solution.py:132
  54.3 1.1 copy-done.2
  55.4 3.7 %all-to-all-start.1 = ((bf16[16,3,16,896]{3,2,1,0:T(8,128)(2,1)}), bf16[16,3,16,896]{3,2,1,0:T(8,128)(2,1)S(1)}, u32[]{:S(2)}, u32[]{:S(2)}) async-start(bf16[16,3,16,896]{3,2,1,0:T(8,128)(2,1)} %pack.2), calls=%async_computation.1 | async-start | bytes 2752512 | tf_op jit(solution)/shard_map/all_to_all | solution.py:132
  59.2 1.3 copy-done.3
  60.5 1.4 copy-done.5
  61.9 1.4 copy-done.7
  63.3 23.8 %attend.2 = (bf16[384,2048]{1,0:T(8,128)(2,1)}, bf16[384,2048]{1,0:T(8,128)(2,1)}, bf16[32,3,8,896]{3,2,1,0:T(8,128)(2,1)S(1)}) custom-call(s32[1]{0:T(128)} %bitcast.live_ref, bf16[16,3,16,896]{3,2,1,0:T(8,128)(2,1)S(1)} %copy-done.3, bf16[896,4096]{1,0:T(8,128)(2,1)} %w_ref.3, bf16[384,2048]{1,0:T(8,128)(2,1)S(1)} %bitcast.19, bf16[384,2048]{1,0:T(8,128)(2,1)S(1)} %bitcast.21), custom_call_target="tpu_custom_call" | custom-call | flops 12482248704 | bytes 16777216 | tf_op jit(solution)/shard_map/attend/pallas_call | solution.py:93
  87.1 1.1 copy-done.4
  88.2 7.9 %all-to-all-start.3 = ((bf16[32,3,8,896]{3,2,1,0:T(8,128)(2,1)}), bf16[32,3,8,896]{3,2,1,0:T(8,128)(2,1)}, u32[]{:S(2)}, u32[]{:S(2)}) async-start(bf16[32,3,8,896]{3,2,1,0:T(8,128)(2,1)} %copy-done.4), calls=%async_computation.3 | async-start | bytes 2752512 | tf_op jit(solution)/shard_map/all_to_all | solution.py:132
  96.3 1.4 copy-done.6
  97.7 1.4 copy-done.8
  99.1 23.8 %attend.3 = (bf16[384,2048]{1,0:T(8,128)(2,1)}, bf16[384,2048]{1,0:T(8,128)(2,1)}, bf16[32,3,8,896]{3,2,1,0:T(8,128)(2,1)S(1)}) custom-call(s32[1]{0:T(128)} %bitcast.live_ref, bf16[16,3,16,896]{3,2,1,0:T(8,128)(2,1)S(1)} %all-to-all-done.1.rows_ref, bf16[896,4096]{1,0:T(8,128)(2,1)} %w_ref.3, ...), custom_call_target="tpu_custom_call", output_to_operand_aliasing={{0}: (5, {}), {1}: (6, {})} | custom-call | flops 12482248704 | bytes 16777216 | tf_op jit(solution)/shard_map/attend/pallas_call | solution.py:93
  122.9 1.1 copy-done.1
  124.0 7.1 %all-to-all-start.4 = ((bf16[32,3,8,896]{3,2,1,0:T(8,128)(2,1)}), bf16[32,3,8,896]{3,2,1,0:T(8,128)(2,1)S(1)}, u32[]{:S(2)}, u32[]{:S(2)}) async-start(bf16[32,3,8,896]{3,2,1,0:T(8,128)(2,1)} %copy-done.1), calls=%async_computation.4 | async-start | bytes 2752512 | tf_op jit(solution)/shard_map/all_to_all | solution.py:132
  131.2 21.6 %all_gather.4 = s32[8,4,12]{2,1,0:T(4,128)S(1)} all-gather(s32[1,4,12]{2,1,0:T(4,128)S(1)} %or_select_fusion), channel_id=1, replica_groups=mesh['y'=4,'c'=2,'x'=4,'z'=4] {'y','c'}, dimensions={0}, use_global_device_ids=true | all-gather | bytes 1728 | tf_op jit(solution)/shard_map/all_gather | solution.py:171
  154.0 1.9 %fusion.1 = f32[256,896]{1,0:T(8,128)S(1)} fusion(bf16[768,896]{1,0:T(8,128)(2,1)} %bitcast.8, s32[768]{0:T(1024)S(1)} %eq.31), kind=kOutput, calls=%fused_computation.6 | convolution fusion | flops 352518144 | bytes 2296832 | tf_op jit(solution)/shard_map/dot_general | solution.py:185
  155.9 0.6 fusion
  156.5 20.0 %all_to_all.31 = bf16[16,16,896]{2,1,0:T(8,128)(2,1)S(1)} all-to-all(bf16[16,16,896]{2,1,0:T(8,128)(2,1)S(1)} %bitcast.24), channel_id=1, replica_groups=mesh['y'=4,'c'=2,'x'=4,'z'=4] {'x','z'}, dimensions={0} | all-to-all | bytes 917504 | tf_op jit(solution)/shard_map/all_to_all | solution.py:132
  177.0 0.7 copy.40
  (43 shorter events, 2.5 us)
Async XLA Ops:
  0.6 1.2 copy-start
  0.6 1.3 copy-start.9
  30.5 23.8 %all-to-all-start.2 = ((bf16[16,3,16,896]{3,2,1,0:T(8,128)(2,1)}), bf16[16,3,16,896]{3,2,1,0:T(8,128)(2,1)S(1)}, u32[]{:S(2)}, u32[]{:S(2)}) async-start(bf16[16,3,16,896]{3,2,1,0:T(8,128)(2,1)} %pack.3), calls=%async_computation.2 | async-start | bytes 2752512 | tf_op jit(solution)/shard_map/all_to_all | solution.py:132
  54.3 1.1 copy-start.2
  55.4 32.8 %all-to-all-start.1 = ((bf16[16,3,16,896]{3,2,1,0:T(8,128)(2,1)}), bf16[16,3,16,896]{3,2,1,0:T(8,128)(2,1)S(1)}, u32[]{:S(2)}, u32[]{:S(2)}) async-start(bf16[16,3,16,896]{3,2,1,0:T(8,128)(2,1)} %pack.2), calls=%async_computation.1 | async-start | bytes 2752512 | tf_op jit(solution)/shard_map/all_to_all | solution.py:132
  59.1 1.3 copy-start.3
  60.5 1.4 copy-start.5
  61.9 1.4 copy-start.7
  87.1 1.1 copy-start.4
  88.2 35.8 %all-to-all-start.3 = ((bf16[32,3,8,896]{3,2,1,0:T(8,128)(2,1)}), bf16[32,3,8,896]{3,2,1,0:T(8,128)(2,1)}, u32[]{:S(2)}, u32[]{:S(2)}) async-start(bf16[32,3,8,896]{3,2,1,0:T(8,128)(2,1)} %copy-done.4), calls=%async_computation.3 | async-start | bytes 2752512 | tf_op jit(solution)/shard_map/all_to_all | solution.py:132
  96.3 1.4 copy-start.6
  97.7 1.4 copy-start.8
  122.9 1.1 copy-start.1
  124.0 32.0 %all-to-all-start.4 = ((bf16[32,3,8,896]{3,2,1,0:T(8,128)(2,1)}), bf16[32,3,8,896]{3,2,1,0:T(8,128)(2,1)S(1)}, u32[]{:S(2)}, u32[]{:S(2)}) async-start(bf16[32,3,8,896]{3,2,1,0:T(8,128)(2,1)} %copy-done.1), calls=%async_computation.4 | async-start | bytes 2752512 | tf_op jit(solution)/shard_map/all_to_all | solution.py:132
where the time goes:
time: 179 us; the launch traced here: 178 us
  blocking collectives  67.5 us (38%)
  Pallas kernels  51.8 us (29%)
  starting transfers between devices  22.5 us (13%)
  waiting for transfers between devices  18 us (10%)
  local copies, waits for them, and re-layouts  13.4 us (7%)
  matrix products  2.51 us (1%)
    pallas_call x2, Pallas kernels, attend(): pl.pallas_call(functools.partial(attend_kernel, width // HD, first_group)...  47.6 us
    all_to_all x2, blocking collectives, exchange(): return lax.all_to_all(block, axes, split_axis=0, concat_axis=0, tiled=True)  45.9 us
    all_to_all x4, starting transfers between devices, exchange(): return lax.all_to_all(block, axes, split_axis=0, concat_axis=0, tiled=True)  22.5 us
    all_gather x1, blocking collectives, body(): lax.all_gather(column, DP, axis=0, tiled=False)  21.6 us
    all_to_all x4, waiting for transfers between devices, exchange(): return lax.all_to_all(block, axes, split_axis=0, concat_axis=0, tiled=True)  18 us
    unnamed x21, local copies, waits for them, and re-layouts  12.1 us
    pallas_call x2, Pallas kernels, pack(): pl.pallas_call(functools.partial(pack_kernel, first_group, group_count, c...  4.22 us
  transfers between devices with their start and end apart: 4, of which 1 were waited for; matrix products, arithmetic and copies ran while one was open for 2% of the time, Pallas kernels for 28%

commit v1 on v0

--- a/solution.py
+++ b/solution.py
@@ -14,7 +14,8 @@
 DP = ("y", "c")
 LINE = ("y", "c", "x")
 CHUNKS = 2
-HEAD_BATCH = 8
+HEAD_BATCH = 4
+LANES = 128
 F32 = jnp.float32
 BF16 = jnp.bfloat16
 
@@ -23,23 +24,26 @@
     return lax.dot_general(a, b, (((ca,), (cb,)), ((), ())), preferred_element_type=F32)
 
 
-def pack_kernel(first_group, group_count, chunk_groups, ids_ref, table_ref, out_ref):
+def pack_kernel(first_group, group_count, chunk_groups, lane_tiles, ids_ref, table_ref, out_ref):
     def per_dest(dest, carry):
         for g in range(chunk_groups):
             at = dest * 2 * group_count + 2 * (first_group + g)
             first, second = ids_ref[at], ids_ref[at + 1]
-            a = table_ref[first >> 2, first & 3].astype(F32)
-            b = table_ref[second >> 2, second & 3].astype(F32)
-            out_ref[dest, g] = jnp.concatenate([a[:4], b[:4], a[4:], b[4:]], axis=0).astype(BF16)
+            for t in range(lane_tiles):
+                a = table_ref[first >> 2, (first & 3) * lane_tiles + t].astype(F32)
+                b = table_ref[second >> 2, (second & 3) * lane_tiles + t].astype(F32)
+                out_ref[dest, g, :, t * LANES : (t + 1) * LANES] = jnp.concatenate(
+                    [a[:4], b[:4], a[4:], b[4:]], axis=0
+                ).astype(BF16)
         return carry
 
     lax.fori_loop(0, out_ref.shape[0], per_dest, 0)
 
 
-def pack(ids, table, first_group, group_count, chunk_groups):
-    dests, enc = table.shape[0], table.shape[-1]
+def pack(ids, table, enc, first_group, group_count, chunk_groups):
+    dests = table.shape[0]
     return pl.pallas_call(
-        functools.partial(pack_kernel, first_group, group_count, chunk_groups),
+        functools.partial(pack_kernel, first_group, group_count, chunk_groups, enc // LANES),
         out_shape=jax.ShapeDtypeStruct((dests, chunk_groups, 16, enc), BF16),
         in_specs=[
             pl.BlockSpec(memory_space=pltpu.SMEM),
@@ -51,23 +55,30 @@
     )(ids, table)
 
 
-def attend_kernel(
-    heads, first_group, live_ref, rows_ref, w_ref, q_ref, g_ref, *rest
-):
+def attend_kernel(heads, first_group, live_ref, rows_ref, w_ref, q_ref, g_ref, *rest):
     att_ref, qg_ref, term_ref, kv, kv_grad, q_turned, g_turned = rest[-7:]
     scale = HD**-0.5
     width = heads * HD
-    live = (live_ref[0] > 0) | (pl.program_id(0) + first_group > 0)
-    rows = rows_ref[...].reshape(-1, rows_ref.shape[-1])
-    kv[...] = dot(rows, w_ref[...], 1, 0).astype(BF16)
+    step = pl.program_id(0)
+    live = (live_ref[0] > 0) | (step + first_group > 0)
     grads = jnp.where(live, g_ref[...], jnp.zeros((), BF16))
     q_turned[...] = jnp.transpose(q_ref[...])
     g_turned[...] = jnp.transpose(grads)
+
+    def project(base):
+        rows = rows_ref[:, step].reshape(-1, rows_ref.shape[-1])
+        for start in (base * HD, width + base * HD):
+            part = slice(start, start + HEAD_BATCH * HD)
+            kv[:, part] = dot(rows, w_ref[:, part], 1, 0).astype(BF16)
+
+    project(0)
     for base in range(0, heads, HEAD_BATCH):
         keys = [slice(h * HD, (h + 1) * HD) for h in range(base, base + HEAD_BATCH)]
         values = [slice(width + h * HD, width + (h + 1) * HD) for h in range(base, base + HEAD_BATCH)]
         scores = [dot(q_ref[:, k], kv[:, k], 1, 1) * scale for k in keys]
         grad_probs = [dot(grads[:, k], kv[:, v], 1, 1) for k, v in zip(keys, values)]
+        if base + HEAD_BATCH < heads:
+            project(base + HEAD_BATCH)
         raised = [jnp.exp(s - jnp.max(s, axis=-1, keepdims=True)) for s in scores]
         probs = [e / jnp.sum(e, axis=-1, keepdims=True) for e in raised]
         halves = [p.astype(BF16) for p in probs]
@@ -84,6 +95,10 @@
     term_ref[...] = terms.reshape(term_ref.shape)
 
 
+def in_hbm(*arrays):
+    return [pltpu.with_memory_space_constraint(a, pltpu.HBM) for a in arrays]
+
+
 def attend(live, rows, weight, queries, grads, before, first_group, line):
     slices, chunk_groups, _, enc = rows.shape
     tokens, width = queries.shape
@@ -93,16 +108,16 @@
     return pl.pallas_call(
         functools.partial(attend_kernel, width // HD, first_group),
         out_shape=[
-            jax.ShapeDtypeStruct((tokens, width), BF16),
-            jax.ShapeDtypeStruct((tokens, width), BF16),
-            jax.ShapeDtypeStruct((line, chunk_groups, keys // line, enc), BF16),
+            pltpu.HBM((tokens, width), BF16),
+            pltpu.HBM((tokens, width), BF16),
+            pltpu.HBM((line, chunk_groups, keys // line, enc), BF16),
         ],
         grid_spec=pltpu.PrefetchScalarGridSpec(
             num_scalar_prefetch=1,
             grid=(chunk_groups,),
             in_specs=[
-                pl.BlockSpec((slices, 1, 16, enc), lambda i, l: (0, i, 0, 0)),
-                pl.BlockSpec((enc, 2 * width), lambda i, l: (0, 0)),
+                pl.BlockSpec(memory_space=pltpu.VMEM),
+                pl.BlockSpec(weight.shape, lambda i, l: (0, 0), pipeline_mode=pl.Buffered(1)),
                 block,
                 block,
             ]
@@ -120,12 +135,10 @@
             ],
         ),
         input_output_aliases={5 + n: n for n in range(len(before))},
-        cost_estimate=pl.CostEstimate(
-            flops=flops, bytes_accessed=16 << 20, transcendentals=0
-        ),
-        compiler_params=pltpu.CompilerParams(vmem_limit_bytes=44 << 20),
+        cost_estimate=pl.CostEstimate(flops=flops, bytes_accessed=16 << 20, transcendentals=0),
+        compiler_params=pltpu.CompilerParams(vmem_limit_bytes=32 << 20),
         name="attend",
-    )(live, rows, weight, queries, grads, *before)
+    )(live, rows, *in_hbm(weight, queries, grads, *before))
 
 
 def exchange(block, axes):
@@ -145,20 +158,22 @@
     chunk_groups = group_count // CHUNKS
     own_tokens = row_tokens // line
 
-    slices = database.reshape(held, seq_count, row_tokens // seq_count, enc).transpose(1, 0, 2, 3)
-    id_rows = jnp.pad(
-        neighbours.reshape(1, ref_count).astype(BF16), ((0, row_tokens // seq_count - 1), (0, enc - ref_count))
-    )
-    id_rows = jnp.broadcast_to(id_rows[None, None], (seq_count, 1) + id_rows.shape)
-    table = exchange(jnp.concatenate([slices, id_rows], axis=1), SEQ)
-    all_ids = table[:, held, 0, :ref_count].astype(jnp.int32).reshape(-1)
+    slice_rows, lane_tiles = row_tokens // seq_count, enc // LANES
+    slices = database.reshape(held, seq_count, slice_rows, lane_tiles, LANES)
+    slices = slices.transpose(1, 0, 3, 2, 4).reshape(seq_count, held * lane_tiles, slice_rows, LANES)
+    id_tile = jnp.pad(
+        neighbours.reshape(1, ref_count).astype(BF16), ((0, slice_rows - 1), (0, LANES - ref_count))
+    )
+    id_tile = jnp.broadcast_to(id_tile, (seq_count, 1, slice_rows, LANES))
+    table = exchange(jnp.concatenate([slices, id_tile], axis=1), SEQ)
+    all_ids = table[:, held * lane_tiles, 0, :ref_count].astype(jnp.int32).reshape(-1)
     windows = jnp.concatenate([all_ids[:2], all_ids[:-2]])
 
     live = (seq_index > 0).astype(jnp.int32).reshape(1)
-    rows = [
-        exchange(pack(windows, table, c * chunk_groups, group_count, chunk_groups), SEQ)
-        for c in range(CHUNKS)
+    packed = [
+        pack(windows, table, enc, c * chunk_groups, group_count, chunk_groups) for c in range(CHUNKS)
     ]
+    rows = [exchange(p, SEQ) for p in packed]
 
     z_index = lax.axis_index("z")
     column = lax.dynamic_index_in_dim(
@@ -168,21 +183,30 @@
         (jnp.arange(x_count)[:, None] > 0) | (z_index > 0) | (jnp.arange(ref_count)[None, :] >= 2)
     )
     column = jnp.where(column_live, column, -1)
+    column, _ = lax.optimization_barrier((column, packed[-1]))
     line_ids = lax.all_gather(column, DP, axis=0, tiled=False).reshape(line, group_count, 2)
     keys = jnp.where(
         line_ids[..., None] >= 0, line_ids[..., None] * own_tokens + jnp.arange(own_tokens), -1
     )
 
+    slots = seq_count * held * own_tokens
+    matches = [
+        (
+            jnp.arange(slots)[:, None]
+            == keys[:, c * chunk_groups : (c + 1) * chunk_groups].reshape(1, -1)
+        ).astype(BF16)
+        for c in range(CHUNKS)
+    ]
+    live, matches = lax.optimization_barrier((live, matches))
+
     done = ()
-    total = jnp.zeros((seq_count * held * own_tokens, enc), F32)
+    total = jnp.zeros((slots, enc), F32)
     for c in range(CHUNKS):
         *done, terms = attend(
             live, rows[c], kv_weight, queries[0], out_grad[0], done, c * chunk_groups, line
         )
         back = exchange(terms, LINE)
-        chunk_keys = keys[:, c * chunk_groups : (c + 1) * chunk_groups].reshape(1, -1)
-        match = (jnp.arange(total.shape[0])[:, None] == chunk_keys).astype(BF16)
-        total = total + jnp.dot(match, back.reshape(-1, enc), preferred_element_type=F32)
+        total = total + jnp.dot(matches[c], back.reshape(-1, enc), preferred_element_type=F32)
     owned = exchange(total.astype(BF16).reshape(seq_count, held * own_tokens, enc), SEQ)
     owned = owned.reshape(x_count, z_count, held, own_tokens, enc).astype(F32).sum(axis=1)
     row_grad = owned.transpose(1, 0, 2, 3).reshape(held, x_count * own_tokens, enc)

time: 179 us -> 160 us (0.89)
  blocking collectives: 67.5 us -> 28.3 us
  waiting for transfers between devices: 18 us -> 38.9 us
  local copies, waits for them, and re-layouts: 13.4 us -> 3.21 us
  starting transfers between devices: 22.5 us -> 31 us
    all_to_all x2 -> x1, blocking collectives: 45.9 us -> 16.2 us  [exchange(): return lax.all_to_all(block, axes, split_axis=0, concat_axis=0, tiled=True)]
    all_to_all x4 -> x5, waiting for transfers between devices: 18 us -> 38.9 us  [exchange(): return lax.all_to_all(block, axes, split_axis=0, concat_axis=0, tiled=True)]
    unnamed x21 -> x3, local copies, waits for them, and re-layouts: 12.1 us -> 0.71 us
    all_gather x1, blocking collectives: 21.6 us -> 12.1 us  [body(): lax.all_gather(column, DP, axis=0, tiled=False)]
    all_to_all x4 -> x5, starting transfers between devices: 22.5 us -> 31 us  [exchange(): return lax.all_to_all(block, axes, split_axis=0, concat_axis=0, tiled=True)]
  transfers between devices with their start and end apart: 4 -> 5, of which waited for: 1 -> 3; matrix products, arithmetic and copies ran while one was open for 2% -> 2% of each run, Pallas kernels for 28% -> 31%
where the time goes in v1:
time: 160 us
  Pallas kernels  51.8 us (32%)
  waiting for transfers between devices  38.9 us (24%)
  starting transfers between devices  31 us (19%)
  blocking collectives  28.3 us (18%)
  matrix products  3.27 us (2%)
  local copies, waits for them, and re-layouts  3.21 us (2%)
  other arithmetic  2.22 us (1%)
    pallas_call x2, Pallas kernels, attend(): pl.pallas_call(functools.partial(attend_kernel, width // HD, first_group)...  47.5 us
    all_to_all x5, waiting for transfers between devices, exchange(): return lax.all_to_all(block, axes, split_axis=0, concat_axis=0, tiled=True)  38.9 us
    all_to_all x5, starting transfers between devices, exchange(): return lax.all_to_all(block, axes, split_axis=0, concat_axis=0, tiled=True)  31 us
    all_to_all x1, blocking collectives, exchange(): return lax.all_to_all(block, axes, split_axis=0, concat_axis=0, tiled=True)  16.2 us
    all_gather x1, blocking collectives, body(): lax.all_gather(column, DP, axis=0, tiled=False)  12.1 us
    pallas_call x2, Pallas kernels, pack(): pl.pallas_call(functools.partial(pack_kernel, first_group, group_count, c...  4.31 us
    dot_general x2, matrix products, body(): jnp.dot(matches[c], back.reshape(-1, enc), preferred_element_type=F32)  3.27 us
  transfers between devices with their start and end apart: 5, of which 3 were waited for; matrix products, arithmetic and copies ran while one was open for 2% of the time, Pallas kernels for 31%

profile of v1, /device:TPU:0, one launch (start us, length us, event | category | flops | bytes accessed | tf_op | source)
XLA Modules:
  0.0 159.5 jit_solution(9683564223451067802)
XLA Ops:
  0.6 1.3 copy.32
  2.1 1.0 pad_maximum_fusion
  3.2 8.0 %all-to-all-start = ((bf16[16,29,8,128]{3,2,1,0:T(8,128)(2,1)}), bf16[16,29,8,128]{3,2,1,0:T(8,128)(2,1)S(1)}, u32[]{:S(2)}, u32[]{:S(2)}) async-start(bf16[16,29,8,128]{3,2,1,0:T(8,128)(2,1)} %pad_maximum_fusion), calls=%async_computation | async-start | bytes 1900544 | tf_op jit(solution)/shard_map/all_to_all | solution.py:145
  11.2 16.4 %all-to-all-done.table_ref = bf16[16,29,8,128]{3,2,1,0:T(8,128)(2,1)S(1)} async-done(((bf16[16,29,8,128]{3,2,1,0:T(8,128)(2,1)}), bf16[16,29,8,128]{3,2,1,0:T(8,128)(2,1)S(1)}, u32[]{:S(2)}, u32[]{:S(2)}) %all-to-all-start) | async-done | bytes 950304 | tf_op jit(solution)/shard_map/all_to_all | solution.py:145
  27.8 2.1 %pack.3 = bf16[16,3,16,896]{3,2,1,0:T(8,128)(2,1)} custom-call(s32[192]{0:T(256)S(1)} %pad_add_fusion.ids_ref, bf16[16,29,8,128]{3,2,1,0:T(8,128)(2,1)S(1)} %all-to-all-done.table_ref), custom_call_target="tpu_custom_call" | custom-call | tf_op jit(solution)/shard_map/pack/pallas_call | solution.py:45
  29.9 3.7 %all-to-all-start.2 = ((bf16[16,3,16,896]{3,2,1,0:T(8,128)(2,1)}), bf16[16,3,16,896]{3,2,1,0:T(8,128)(2,1)S(1)}, u32[]{:S(2)}, u32[]{:S(2)}) async-start(bf16[16,3,16,896]{3,2,1,0:T(8,128)(2,1)} %pack.3), calls=%async_computation.2 | async-start | bytes 2752512 | tf_op jit(solution)/shard_map/all_to_all | solution.py:145
  33.8 2.2 %pack.2 = bf16[16,3,16,896]{3,2,1,0:T(8,128)(2,1)} custom-call(s32[192]{0:T(256)S(1)} %pad_add_fusion.ids_ref, bf16[16,29,8,128]{3,2,1,0:T(8,128)(2,1)S(1)} %all-to-all-done.table_ref), custom_call_target="tpu_custom_call" | custom-call | tf_op jit(solution)/shard_map/pack/pallas_call | solution.py:45
  36.0 12.1 %all-gather.1 = s32[8,4,12]{2,1,0:T(4,128)S(1)} all-gather(s32[1,4,12]{2,1,0:T(4,128)S(1)} %bitcast.28), channel_id=2, replica_groups=mesh['y'=4,'c'=2,'x'=4,'z'=4] {'y','c'}, dimensions={0}, use_global_device_ids=true | all-gather | bytes 1728 | tf_op jit(solution)/shard_map/all_gather | solution.py:187
  48.3 0.6 add_select_fusion
  49.1 0.2 eq.35
  49.3 3.5 %all-to-all-done.2.rows_ref = bf16[16,3,16,896]{3,2,1,0:T(8,128)(2,1)S(1)} async-done(((bf16[16,3,16,896]{3,2,1,0:T(8,128)(2,1)}), bf16[16,3,16,896]{3,2,1,0:T(8,128)(2,1)S(1)}, u32[]{:S(2)}, u32[]{:S(2)}) %all-to-all-start.2) | async-done | bytes 1376288 | tf_op jit(solution)/shard_map/all_to_all | solution.py:145
  52.8 4.4 %all-to-all-start.1 = ((bf16[16,3,16,896]{3,2,1,0:T(8,128)(2,1)}), bf16[16,3,16,896]{3,2,1,0:T(8,128)(2,1)}, u32[]{:S(2)}, u32[]{:S(2)}) async-start(bf16[16,3,16,896]{3,2,1,0:T(8,128)(2,1)} %pack.2), calls=%async_computation.1 | async-start | bytes 2752512 | tf_op jit(solution)/shard_map/all_to_all | solution.py:145
  57.2 0.2 fusion.1
  57.4 23.5 %attend.2 = (bf16[384,2048]{1,0:T(8,128)(2,1)}, bf16[384,2048]{1,0:T(8,128)(2,1)}, bf16[32,3,8,896]{3,2,1,0:T(8,128)(2,1)}) custom-call(s32[1]{0:T(128)} %bitcast.live_ref, bf16[16,3,16,896]{3,2,1,0:T(8,128)(2,1)S(1)} %all-to-all-done.2.rows_ref, bf16[896,4096]{1,0:T(8,128)(2,1)} %w_ref.3, bf16[384,2048]{1,0:T(8,128)(2,1)} %bitcast.31, ...), custom_call_target="tpu_custom_call" | custom-call | flops 12482248704 | bytes 16777216 | tf_op jit(solution)/shard_map/attend/pallas_call | solution.py:108
  80.9 7.8 %all-to-all-start.3 = ((bf16[32,3,8,896]{3,2,1,0:T(8,128)(2,1)}), bf16[32,3,8,896]{3,2,1,0:T(8,128)(2,1)S(1)}, u32[]{:S(2)}, u32[]{:S(2)}) async-start(bf16[32,3,8,896]{3,2,1,0:T(8,128)(2,1)} %get-tuple-element.20), calls=%async_computation.3 | async-start | bytes 2752512 | tf_op jit(solution)/shard_map/all_to_all | solution.py:145
  88.7 23.9 %attend.3 = (bf16[384,2048]{1,0:T(8,128)(2,1)}, bf16[384,2048]{1,0:T(8,128)(2,1)}, bf16[32,3,8,896]{3,2,1,0:T(8,128)(2,1)}) custom-call(s32[1]{0:T(128)} %bitcast.live_ref, bf16[16,3,16,896]{3,2,1,0:T(8,128)(2,1)} %all-to-all-done.1.rows_ref, bf16[896,4096]{1,0:T(8,128)(2,1)} %w_ref.3, ...), custom_call_target="tpu_custom_call", output_to_operand_aliasing={{0}: (5, {}), {1}: (6, {})} | custom-call | flops 12482248704 | bytes 16777216 | tf_op jit(solution)/shard_map/attend/pallas_call | solution.py:108
  112.6 7.2 %all-to-all-start.4 = ((bf16[32,3,8,896]{3,2,1,0:T(8,128)(2,1)}), bf16[32,3,8,896]{3,2,1,0:T(8,128)(2,1)S(1)}, u32[]{:S(2)}, u32[]{:S(2)}) async-start(bf16[32,3,8,896]{3,2,1,0:T(8,128)(2,1)} %get-tuple-element.22), calls=%async_computation.4 | async-start | bytes 2752512 | tf_op jit(solution)/shard_map/all_to_all | solution.py:145
  119.8 1.5 fusion.5
  121.3 19.0 %all-to-all-done.4 = bf16[32,3,8,896]{3,2,1,0:T(8,128)(2,1)S(1)} async-done(((bf16[32,3,8,896]{3,2,1,0:T(8,128)(2,1)}), bf16[32,3,8,896]{3,2,1,0:T(8,128)(2,1)S(1)}, u32[]{:S(2)}, u32[]{:S(2)}) %all-to-all-start.4) | async-done | bytes 1376288 | tf_op jit(solution)/shard_map/all_to_all | solution.py:145
  140.3 1.8 %fusion = bf16[256,896]{1,0:T(8,128)(2,1)S(1)} fusion(f32[256,896]{1,0:T(8,128)} %fusion.5, bf16[256,768]{1,0:T(8,128)(2,1)S(1)} %get-tuple-element.21, bf16[768,896]{1,0:T(8,128)(2,1)S(1)} %bitcast.21), kind=kOutput, calls=%fused_computation.1 | convolution fusion | flops 352780288 | bytes 3145728 | tf_op jit(solution)/shard_map/dot_general | solution.py:209
  142.1 16.2 %all_to_all.30 = bf16[16,16,896]{2,1,0:T(8,128)(2,1)S(1)} all-to-all(bf16[16,16,896]{2,1,0:T(8,128)(2,1)S(1)} %bitcast.24), channel_id=1, replica_groups=mesh['y'=4,'c'=2,'x'=4,'z'=4] {'x','z'}, dimensions={0} | all-to-all | bytes 917504 | tf_op jit(solution)/shard_map/all_to_all | solution.py:145
  158.3 0.2 reshape.100
  158.5 0.2 reduce_sum.9
  158.8 0.7 copy.41
  (27 shorter events, 1.1 us)
Async XLA Ops:
  0.6 1.3 copy-start
  3.2 24.4 %all-to-all-start = ((bf16[16,29,8,128]{3,2,1,0:T(8,128)(2,1)}), bf16[16,29,8,128]{3,2,1,0:T(8,128)(2,1)S(1)}, u32[]{:S(2)}, u32[]{:S(2)}) async-start(bf16[16,29,8,128]{3,2,1,0:T(8,128)(2,1)} %pad_maximum_fusion), calls=%async_computation | async-start | bytes 1900544 | tf_op jit(solution)/shard_map/all_to_all | solution.py:145
  29.9 22.8 %all-to-all-start.2 = ((bf16[16,3,16,896]{3,2,1,0:T(8,128)(2,1)}), bf16[16,3,16,896]{3,2,1,0:T(8,128)(2,1)S(1)}, u32[]{:S(2)}, u32[]{:S(2)}) async-start(bf16[16,3,16,896]{3,2,1,0:T(8,128)(2,1)} %pack.3), calls=%async_computation.2 | async-start | bytes 2752512 | tf_op jit(solution)/shard_map/all_to_all | solution.py:145
  52.8 28.1 %all-to-all-start.1 = ((bf16[16,3,16,896]{3,2,1,0:T(8,128)(2,1)}), bf16[16,3,16,896]{3,2,1,0:T(8,128)(2,1)}, u32[]{:S(2)}, u32[]{:S(2)}) async-start(bf16[16,3,16,896]{3,2,1,0:T(8,128)(2,1)} %pack.2), calls=%async_computation.1 | async-start | bytes 2752512 | tf_op jit(solution)/shard_map/all_to_all | solution.py:145
  80.9 31.7 %all-to-all-start.3 = ((bf16[32,3,8,896]{3,2,1,0:T(8,128)(2,1)}), bf16[32,3,8,896]{3,2,1,0:T(8,128)(2,1)S(1)}, u32[]{:S(2)}, u32[]{:S(2)}) async-start(bf16[32,3,8,896]{3,2,1,0:T(8,128)(2,1)} %get-tuple-element.20), calls=%async_computation.3 | async-start | bytes 2752512 | tf_op jit(solution)/shard_map/all_to_all | solution.py:145
  112.6 27.7 %all-to-all-start.4 = ((bf16[32,3,8,896]{3,2,1,0:T(8,128)(2,1)}), bf16[32,3,8,896]{3,2,1,0:T(8,128)(2,1)S(1)}, u32[]{:S(2)}, u32[]{:S(2)}) async-start(bf16[32,3,8,896]{3,2,1,0:T(8,128)(2,1)} %get-tuple-element.22), calls=%async_computation.4 | async-start | bytes 2752512 | tf_op jit(solution)/shard_map/all_to_all | solution.py:145

commit v2 on v1

--- a/solution.py
+++ b/solution.py
@@ -24,14 +24,56 @@
     return lax.dot_general(a, b, (((ca,), (cb,)), ((), ())), preferred_element_type=F32)
 
 
-def pack_kernel(first_group, group_count, chunk_groups, lane_tiles, ids_ref, table_ref, out_ref):
+def spread_kernel(core_ref, ids_ref, rows_ref, out_ref):
+    half, tokens, enc = rows_ref.shape
+    lane_tiles = enc // LANES
+    lanes = lax.broadcasted_iota(jnp.int32, (8, LANES), 1)
+    ids = jnp.zeros((8, LANES), jnp.int32)
+    for r in range(ids_ref.shape[0]):
+        ids = jnp.where(lanes == r, ids_ref[r], ids)
+    ids = ids.astype(F32).astype(BF16)
+    for pair in range(tokens // 16):
+        for j in range(half):
+            for t in range(lane_tiles):
+                rows = rows_ref[j, 16 * pair : 16 * pair + 16, t * LANES : (t + 1) * LANES].astype(F32)
+                out_ref[2 * pair, j * lane_tiles + t] = rows[:8].astype(BF16)
+                out_ref[2 * pair + 1, j * lane_tiles + t] = rows[8:].astype(BF16)
+        out_ref[2 * pair, half * lane_tiles] = ids
+        out_ref[2 * pair + 1, half * lane_tiles] = ids
+
+
+def spread(core, ids, database, dests):
+    held, tokens, enc = database.shape
+    half = held // 2
+    out = (dests, half * (enc // LANES) + 1, tokens // dests, LANES)
+    return pl.pallas_call(
+        spread_kernel,
+        out_shape=pltpu.HBM(out, BF16),
+        grid_spec=pltpu.PrefetchScalarGridSpec(
+            num_scalar_prefetch=2,
+            grid=(1,),
+            in_specs=[pl.BlockSpec((half, tokens, enc), lambda i, core, ids: (core[0], 0, 0))],
+            out_specs=pl.BlockSpec(out, lambda i, core, ids: (0, 0, 0, 0)),
+        ),
+        compiler_params=pltpu.CompilerParams(vmem_limit_bytes=16 << 20),
+        name="spread",
+    )(core, ids, *in_hbm(database))
+
+
+def pack_kernel(
+    first_group, group_count, chunk_groups, lane_tiles, core_ref, ids_ref, own_ref, other_ref, out_ref
+):
+    def load(ref_id, t):
+        at = (ref_id >> 2, (ref_id & 1) * lane_tiles + t)
+        own = ((ref_id >> 1) & 1) == core_ref[0]
+        return jnp.where(own, own_ref[at].astype(F32), other_ref[at].astype(F32))
+
     def per_dest(dest, carry):
         for g in range(chunk_groups):
             at = dest * 2 * group_count + 2 * (first_group + g)
             first, second = ids_ref[at], ids_ref[at + 1]
             for t in range(lane_tiles):
-                a = table_ref[first >> 2, (first & 3) * lane_tiles + t].astype(F32)
-                b = table_ref[second >> 2, (second & 3) * lane_tiles + t].astype(F32)
+                a, b = load(first, t), load(second, t)
                 out_ref[dest, g, :, t * LANES : (t + 1) * LANES] = jnp.concatenate(
                     [a[:4], b[:4], a[4:], b[4:]], axis=0
                 ).astype(BF16)
@@ -40,19 +82,21 @@
     lax.fori_loop(0, out_ref.shape[0], per_dest, 0)
 
 
-def pack(ids, table, enc, first_group, group_count, chunk_groups):
-    dests = table.shape[0]
+def pack(core, ids, own, other, enc, first_group, group_count, chunk_groups):
+    dests = own.shape[0]
     return pl.pallas_call(
         functools.partial(pack_kernel, first_group, group_count, chunk_groups, enc // LANES),
         out_shape=jax.ShapeDtypeStruct((dests, chunk_groups, 16, enc), BF16),
         in_specs=[
             pl.BlockSpec(memory_space=pltpu.SMEM),
+            pl.BlockSpec(memory_space=pltpu.SMEM),
+            pl.BlockSpec(memory_space=pltpu.VMEM),
             pl.BlockSpec(memory_space=pltpu.VMEM),
         ],
         out_specs=pl.BlockSpec(memory_space=pltpu.VMEM),
         compiler_params=pltpu.CompilerParams(vmem_limit_bytes=16 << 20),
         name="pack",
-    )(ids, table)
+    )(core, ids, own, other)
 
 
 def attend_kernel(heads, first_group, live_ref, rows_ref, w_ref, q_ref, g_ref, *rest):
@@ -158,20 +202,17 @@
     chunk_groups = group_count // CHUNKS
     own_tokens = row_tokens // line
 
-    slice_rows, lane_tiles = row_tokens // seq_count, enc // LANES
-    slices = database.reshape(held, seq_count, slice_rows, lane_tiles, LANES)
-    slices = slices.transpose(1, 0, 3, 2, 4).reshape(seq_count, held * lane_tiles, slice_rows, LANES)
-    id_tile = jnp.pad(
-        neighbours.reshape(1, ref_count).astype(BF16), ((0, slice_rows - 1), (0, LANES - ref_count))
-    )
-    id_tile = jnp.broadcast_to(id_tile, (seq_count, 1, slice_rows, LANES))
-    table = exchange(jnp.concatenate([slices, id_tile], axis=1), SEQ)
-    all_ids = table[:, held * lane_tiles, 0, :ref_count].astype(jnp.int32).reshape(-1)
+    core = lax.axis_index("c").astype(jnp.int32).reshape(1)
+    own = exchange(spread(core, neighbours.reshape(ref_count), database, seq_count), SEQ)
+    other = lax.ppermute(own, "c", [(0, 1), (1, 0)])
+    id_tile = held // 2 * (enc // LANES)
+    all_ids = own[:, id_tile, 0, :ref_count].astype(jnp.int32).reshape(-1)
     windows = jnp.concatenate([all_ids[:2], all_ids[:-2]])
 
     live = (seq_index > 0).astype(jnp.int32).reshape(1)
     packed = [
-        pack(windows, table, enc, c * chunk_groups, group_count, chunk_groups) for c in range(CHUNKS)
+        pack(core, windows, own, other, enc, c * chunk_groups, group_count, chunk_groups)
+        for c in range(CHUNKS)
     ]
     rows = [exchange(p, SEQ) for p in packed]
 

time: 160 us -> 161 us (level)
  blocking collectives: 28.3 us -> 47.4 us
  waiting for transfers between devices: 38.9 us -> 27.1 us
  starting transfers between devices: 31 us -> 23.1 us
  Pallas kernels: 51.8 us -> 54.7 us
    all_to_all x1 -> x2, blocking collectives: 16.2 us -> 35.3 us  [exchange(): return lax.all_to_all(block, axes, split_axis=0, concat_axis=0, tiled=True)]
    all_to_all x5 -> x4, waiting for transfers between devices: 38.9 us -> 25.4 us  [exchange(): return lax.all_to_all(block, axes, split_axis=0, concat_axis=0, tiled=True)]
    all_to_all x5 -> x4, starting transfers between devices: 31 us -> 23.1 us  [exchange(): return lax.all_to_all(block, axes, split_axis=0, concat_axis=0, tiled=True)]
    pallas_call x0 -> x1, Pallas kernels: none -> 2.42 us  [spread(): pl.pallas_call(spread_kernel, out_shape=pltpu.HBM(out, BF16), grid_spec=p...]
    ppermute x0 -> x1, waiting for transfers between devices: none -> 1.65 us  [body(): other = lax.ppermute(own, 'c', [(0, 1), (1, 0)])]
where the time goes in v2:
time: 161 us; the launch traced here: 160 us
  Pallas kernels  54.7 us (34%)
  blocking collectives  47.4 us (29%)
  waiting for transfers between devices  27.1 us (17%)
  starting transfers between devices  23.1 us (14%)
  matrix products  3.28 us (2%)
  local copies, waits for them, and re-layouts  2.59 us (2%)
    pallas_call x2, Pallas kernels, attend(): pl.pallas_call(functools.partial(attend_kernel, width // HD, first_group)...  47.5 us
    all_to_all x2, blocking collectives, exchange(): return lax.all_to_all(block, axes, split_axis=0, concat_axis=0, tiled=True)  35.3 us
    all_to_all x4, waiting for transfers between devices, exchange(): return lax.all_to_all(block, axes, split_axis=0, concat_axis=0, tiled=True)  25.4 us
    all_to_all x4, starting transfers between devices, exchange(): return lax.all_to_all(block, axes, split_axis=0, concat_axis=0, tiled=True)  23.1 us
    all_gather x1, blocking collectives, body(): lax.all_gather(column, DP, axis=0, tiled=False)  12.1 us
    pallas_call x2, Pallas kernels, pack(): pl.pallas_call(functools.partial(pack_kernel, first_group, group_count, c...  4.77 us
    dot_general x2, matrix products, body(): jnp.dot(matches[c], back.reshape(-1, enc), preferred_element_type=F32)  3.28 us
  transfers between devices with their start and end apart: 5, of which 3 were waited for; matrix products, arithmetic and copies ran while one was open for 2% of the time, Pallas kernels for 31%

profile of v2, /device:TPU:0, one launch (start us, length us, event | category | flops | bytes accessed | tf_op | source)
XLA Modules:
  0.0 160.1 jit_solution(14586437026021484871)
XLA Ops:
  0.6 0.8 copy.28
  1.5 2.4 %spread.1 = bf16[16,15,8,128]{3,2,1,0:T(8,128)(2,1)} custom-call(s32[1]{0:T(128)} %bitcast.1.core_ref, s32[12]{0:T(128)S(1)} %reshape.77.ids_ref, bf16[4,128,896]{2,1,0:T(8,128)(2,1)} %rows_ref.1), custom_call_target="tpu_custom_call" | custom-call | tf_op jit(solution)/shard_map/spread/pallas_call | solution.py:49
  3.9 19.1 %all_to_all.30.own_ref = bf16[16,15,8,128]{3,2,1,0:T(8,128)(2,1)S(1)} all-to-all(bf16[16,15,8,128]{3,2,1,0:T(8,128)(2,1)} %spread.1), channel_id=1, replica_groups=mesh['y'=4,'c'=2,'x'=4,'z'=4] {'x','z'}, dimensions={0} | all-to-all | bytes 983040 | tf_op jit(solution)/shard_map/all_to_all | solution.py:189
  23.2 1.6 %collective-permute-done.other_ref = bf16[16,15,8,128]{3,2,1,0:T(8,128)(2,1)S(1)} collective-permute-done((bf16[16,15,8,128]{3,2,1,0:T(8,128)(2,1)S(1)}, bf16[16,15,8,128]{3,2,1,0:T(8,128)(2,1)S(1)}, u32[]{:S(2)}, u32[]{:S(2)}) %collective-permute-start) | collective-permute-done | bytes 491552 | tf_op jit(solution)/shard_map/ppermute | solution.py:207
  24.9 2.4 %pack.3 = bf16[16,3,16,896]{3,2,1,0:T(8,128)(2,1)} custom-call(s32[1]{0:T(128)} %bitcast.1.core_ref, s32[192]{0:T(256)S(1)} %pad_add_fusion.ids_ref, bf16[16,15,8,128]{3,2,1,0:T(8,128)(2,1)S(1)} %all_to_all.30.own_ref, bf16[16,15,8,128]{3,2,1,0:T(8,128)(2,1)S(1)} %collective-permute-done.other_ref), custom_call_target="tpu_custom_call" | custom-call | tf_op jit(solution)/shard_map/pack/pallas_call | solution.py:87
  27.2 3.7 %all-to-all-start.2 = ((bf16[16,3,16,896]{3,2,1,0:T(8,128)(2,1)}), bf16[16,3,16,896]{3,2,1,0:T(8,128)(2,1)S(1)}, u32[]{:S(2)}, u32[]{:S(2)}) async-start(bf16[16,3,16,896]{3,2,1,0:T(8,128)(2,1)} %pack.3), calls=%async_computation.2 | async-start | bytes 2752512 | tf_op jit(solution)/shard_map/all_to_all | solution.py:189
  31.2 2.4 %pack.2 = bf16[16,3,16,896]{3,2,1,0:T(8,128)(2,1)} custom-call(s32[1]{0:T(128)} %bitcast.1.core_ref, s32[192]{0:T(256)S(1)} %pad_add_fusion.ids_ref, bf16[16,15,8,128]{3,2,1,0:T(8,128)(2,1)S(1)} %all_to_all.30.own_ref, bf16[16,15,8,128]{3,2,1,0:T(8,128)(2,1)S(1)} %collective-permute-done.other_ref), custom_call_target="tpu_custom_call" | custom-call | tf_op jit(solution)/shard_map/pack/pallas_call | solution.py:87
  33.6 12.1 %all-gather.1 = s32[8,4,12]{2,1,0:T(4,128)S(1)} all-gather(s32[1,4,12]{2,1,0:T(4,128)S(1)} %bitcast.23), channel_id=2, replica_groups=mesh['y'=4,'c'=2,'x'=4,'z'=4] {'y','c'}, dimensions={0}, use_global_device_ids=true | all-gather | bytes 1728 | tf_op jit(solution)/shard_map/all_gather | solution.py:228
  45.9 0.6 add_select_fusion
  46.7 0.2 eq.35
  46.9 6.4 %all-to-all-done.2.rows_ref = bf16[16,3,16,896]{3,2,1,0:T(8,128)(2,1)S(1)} async-done(((bf16[16,3,16,896]{3,2,1,0:T(8,128)(2,1)}), bf16[16,3,16,896]{3,2,1,0:T(8,128)(2,1)S(1)}, u32[]{:S(2)}, u32[]{:S(2)}) %all-to-all-start.2) | async-done | bytes 1376288 | tf_op jit(solution)/shard_map/all_to_all | solution.py:189
  53.3 4.4 %all-to-all-start.1 = ((bf16[16,3,16,896]{3,2,1,0:T(8,128)(2,1)}), bf16[16,3,16,896]{3,2,1,0:T(8,128)(2,1)}, u32[]{:S(2)}, u32[]{:S(2)}) async-start(bf16[16,3,16,896]{3,2,1,0:T(8,128)(2,1)} %pack.2), calls=%async_computation.1 | async-start | bytes 2752512 | tf_op jit(solution)/shard_map/all_to_all | solution.py:189
  57.7 0.2 fusion.1
  57.9 23.5 %attend.2 = (bf16[384,2048]{1,0:T(8,128)(2,1)}, bf16[384,2048]{1,0:T(8,128)(2,1)}, bf16[32,3,8,896]{3,2,1,0:T(8,128)(2,1)}) custom-call(s32[1]{0:T(128)} %bitcast.live_ref, bf16[16,3,16,896]{3,2,1,0:T(8,128)(2,1)S(1)} %all-to-all-done.2.rows_ref, bf16[896,4096]{1,0:T(8,128)(2,1)} %w_ref.3, bf16[384,2048]{1,0:T(8,128)(2,1)} %bitcast.26, ...), custom_call_target="tpu_custom_call" | custom-call | flops 12482248704 | bytes 16777216 | tf_op jit(solution)/shard_map/attend/pallas_call | solution.py:152
  81.4 7.8 %all-to-all-start.3 = ((bf16[32,3,8,896]{3,2,1,0:T(8,128)(2,1)}), bf16[32,3,8,896]{3,2,1,0:T(8,128)(2,1)S(1)}, u32[]{:S(2)}, u32[]{:S(2)}) async-start(bf16[32,3,8,896]{3,2,1,0:T(8,128)(2,1)} %get-tuple-element.20), calls=%async_computation.3 | async-start | bytes 2752512 | tf_op jit(solution)/shard_map/all_to_all | solution.py:189
  89.2 24.0 %attend.3 = (bf16[384,2048]{1,0:T(8,128)(2,1)}, bf16[384,2048]{1,0:T(8,128)(2,1)}, bf16[32,3,8,896]{3,2,1,0:T(8,128)(2,1)}) custom-call(s32[1]{0:T(128)} %bitcast.live_ref, bf16[16,3,16,896]{3,2,1,0:T(8,128)(2,1)} %all-to-all-done.1.rows_ref, bf16[896,4096]{1,0:T(8,128)(2,1)} %w_ref.3, ...), custom_call_target="tpu_custom_call", output_to_operand_aliasing={{0}: (5, {}), {1}: (6, {})} | custom-call | flops 12482248704 | bytes 16777216 | tf_op jit(solution)/shard_map/attend/pallas_call | solution.py:152
  113.2 7.2 %all-to-all-start.4 = ((bf16[32,3,8,896]{3,2,1,0:T(8,128)(2,1)}), bf16[32,3,8,896]{3,2,1,0:T(8,128)(2,1)S(1)}, u32[]{:S(2)}, u32[]{:S(2)}) async-start(bf16[32,3,8,896]{3,2,1,0:T(8,128)(2,1)} %get-tuple-element.22), calls=%async_computation.4 | async-start | bytes 2752512 | tf_op jit(solution)/shard_map/all_to_all | solution.py:189
  120.4 1.5 fusion.5
  121.9 19.0 %all-to-all-done.4 = bf16[32,3,8,896]{3,2,1,0:T(8,128)(2,1)S(1)} async-done(((bf16[32,3,8,896]{3,2,1,0:T(8,128)(2,1)}), bf16[32,3,8,896]{3,2,1,0:T(8,128)(2,1)S(1)}, u32[]{:S(2)}, u32[]{:S(2)}) %all-to-all-start.4) | async-done | bytes 1376288 | tf_op jit(solution)/shard_map/all_to_all | solution.py:189
  140.9 1.8 %fusion = bf16[256,896]{1,0:T(8,128)(2,1)S(1)} fusion(f32[256,896]{1,0:T(8,128)} %fusion.5, bf16[256,768]{1,0:T(8,128)(2,1)S(1)} %get-tuple-element.21, bf16[768,896]{1,0:T(8,128)(2,1)S(1)} %bitcast.18), kind=kOutput, calls=%fused_computation.1 | convolution fusion | flops 352780288 | bytes 3145728 | tf_op jit(solution)/shard_map/dot_general | solution.py:250
  142.6 16.2 %all_to_all.31 = bf16[16,16,896]{2,1,0:T(8,128)(2,1)S(1)} all-to-all(bf16[16,16,896]{2,1,0:T(8,128)(2,1)S(1)} %bitcast.20), channel_id=1, replica_groups=mesh['y'=4,'c'=2,'x'=4,'z'=4] {'x','z'}, dimensions={0} | all-to-all | bytes 917504 | tf_op jit(solution)/shard_map/all_to_all | solution.py:189
  158.9 0.2 reshape.86
  159.1 0.2 reduce_sum.9
  159.4 0.7 copy.36
  (22 shorter events, 0.9 us)
Async XLA Ops:
  23.0 1.9 %collective-permute-start = (bf16[16,15,8,128]{3,2,1,0:T(8,128)(2,1)S(1)}, bf16[16,15,8,128]{3,2,1,0:T(8,128)(2,1)S(1)}, u32[]{:S(2)}, u32[]{:S(2)}) collective-permute-start(bf16[16,15,8,128]{3,2,1,0:T(8,128)(2,1)S(1)} %all_to_all.30.own_ref), channel_id=1, source_target_pairs={{0,16},{16,0},{1,17},{17,1},{2,18},{18,2},{3,19},{19,3},{4,20},{20... | collective-permute-start | bytes 1474568 | tf_op jit(solution)/shard_map/ppermute | solution.py:207
  27.2 26.0 %all-to-all-start.2 = ((bf16[16,3,16,896]{3,2,1,0:T(8,128)(2,1)}), bf16[16,3,16,896]{3,2,1,0:T(8,128)(2,1)S(1)}, u32[]{:S(2)}, u32[]{:S(2)}) async-start(bf16[16,3,16,896]{3,2,1,0:T(8,128)(2,1)} %pack.3), calls=%async_computation.2 | async-start | bytes 2752512 | tf_op jit(solution)/shard_map/all_to_all | solution.py:189
  53.3 28.1 %all-to-all-start.1 = ((bf16[16,3,16,896]{3,2,1,0:T(8,128)(2,1)}), bf16[16,3,16,896]{3,2,1,0:T(8,128)(2,1)}, u32[]{:S(2)}, u32[]{:S(2)}) async-start(bf16[16,3,16,896]{3,2,1,0:T(8,128)(2,1)} %pack.2), calls=%async_computation.1 | async-start | bytes 2752512 | tf_op jit(solution)/shard_map/all_to_all | solution.py:189
  81.4 31.8 %all-to-all-start.3 = ((bf16[32,3,8,896]{3,2,1,0:T(8,128)(2,1)}), bf16[32,3,8,896]{3,2,1,0:T(8,128)(2,1)S(1)}, u32[]{:S(2)}, u32[]{:S(2)}) async-start(bf16[32,3,8,896]{3,2,1,0:T(8,128)(2,1)} %get-tuple-element.20), calls=%async_computation.3 | async-start | bytes 2752512 | tf_op jit(solution)/shard_map/all_to_all | solution.py:189
  113.2 27.7 %all-to-all-start.4 = ((bf16[32,3,8,896]{3,2,1,0:T(8,128)(2,1)}), bf16[32,3,8,896]{3,2,1,0:T(8,128)(2,1)S(1)}, u32[]{:S(2)}, u32[]{:S(2)}) async-start(bf16[32,3,8,896]{3,2,1,0:T(8,128)(2,1)} %get-tuple-element.22), calls=%async_computation.4 | async-start | bytes 2752512 | tf_op jit(solution)/shard_map/all_to_all | solution.py:189

commit v3 on v2

--- a/solution.py
+++ b/solution.py
@@ -12,9 +12,9 @@
 GROUP = 64
 SEQ = ("x", "z")
 DP = ("y", "c")
-LINE = ("y", "c", "x")
+LINE = ("y", "x")
 CHUNKS = 2
-HEAD_BATCH = 4
+HEAD_BATCH = 8
 LANES = 128
 F32 = jnp.float32
 BF16 = jnp.bfloat16
@@ -29,17 +29,21 @@
     lane_tiles = enc // LANES
     lanes = lax.broadcasted_iota(jnp.int32, (8, LANES), 1)
     ids = jnp.zeros((8, LANES), jnp.int32)
-    for r in range(ids_ref.shape[0]):
-        ids = jnp.where(lanes == r, ids_ref[r], ids)
+    for g in range(ids_ref.shape[1]):
+        for r in range(2):
+            ids = jnp.where(lanes == 2 * g + r, ids_ref[r, g], ids)
     ids = ids.astype(F32).astype(BF16)
-    for pair in range(tokens // 16):
+    for y in range(tokens // 32):
         for j in range(half):
             for t in range(lane_tiles):
-                rows = rows_ref[j, 16 * pair : 16 * pair + 16, t * LANES : (t + 1) * LANES].astype(F32)
-                out_ref[2 * pair, j * lane_tiles + t] = rows[:8].astype(BF16)
-                out_ref[2 * pair + 1, j * lane_tiles + t] = rows[8:].astype(BF16)
-        out_ref[2 * pair, half * lane_tiles] = ids
-        out_ref[2 * pair + 1, half * lane_tiles] = ids
+                lane = slice(t * LANES, (t + 1) * LANES)
+                a = rows_ref[j, 32 * y : 32 * y + 16, lane].astype(F32)
+                b = rows_ref[j, 32 * y + 16 : 32 * y + 32, lane].astype(F32)
+                for x in range(4):
+                    piece = jnp.concatenate([a[4 * x : 4 * x + 4], b[4 * x : 4 * x + 4]], axis=0)
+                    out_ref[4 * y + x, j * lane_tiles + t] = piece.astype(BF16)
+    for dest in range(out_ref.shape[0]):
+        out_ref[dest, half * lane_tiles] = ids
 
 
 def spread(core, ids, database, dests):
@@ -57,7 +61,7 @@
         ),
         compiler_params=pltpu.CompilerParams(vmem_limit_bytes=16 << 20),
         name="spread",
-    )(core, ids, *in_hbm(database))
+    )(core, *in_hbm(ids, database))
 
 
 def pack_kernel(
@@ -100,27 +104,45 @@
 
 
 def attend_kernel(heads, first_group, live_ref, rows_ref, w_ref, q_ref, g_ref, *rest):
-    att_ref, qg_ref, term_ref, kv, kv_grad, q_turned, g_turned = rest[-7:]
+    att_ref, qg_ref, term_ref, kv, kv_grad, q_pair, g_pair, q_turned, g_turned = rest[-9:]
     scale = HD**-0.5
     width = heads * HD
+    span = HEAD_BATCH * HD
     step = pl.program_id(0)
     live = (live_ref[0] > 0) | (step + first_group > 0)
+
+    @pl.when(step == 0)
+    def _():
+        for ref in (q_pair, g_pair, q_turned, g_turned):
+            ref[...] = jnp.zeros(ref.shape, BF16)
+
+    queries = q_ref[...]
     grads = jnp.where(live, g_ref[...], jnp.zeros((), BF16))
-    q_turned[...] = jnp.transpose(q_ref[...])
-    g_turned[...] = jnp.transpose(grads)
+    turned = jnp.transpose(queries), jnp.transpose(grads)
+    for h in range(heads):
+        c = slice(h * HD, (h + 1) * HD)
+        r = slice(h * GROUP, (h + 1) * GROUP)
+        in_pair = slice(h % 2 * HD, (h % 2 + 1) * HD)
+        in_four = slice(h % 4 * GROUP, (h % 4 + 1) * GROUP)
+        q_pair[r, in_pair] = queries[:, c]
+        g_pair[r, in_pair] = grads[:, c]
+        q_turned[c, in_four] = turned[0][c]
+        g_turned[c, in_four] = turned[1][c]
 
     def project(base):
         rows = rows_ref[:, step].reshape(-1, rows_ref.shape[-1])
         for start in (base * HD, width + base * HD):
-            part = slice(start, start + HEAD_BATCH * HD)
+            part = slice(start, start + span)
             kv[:, part] = dot(rows, w_ref[:, part], 1, 0).astype(BF16)
 
     project(0)
     for base in range(0, heads, HEAD_BATCH):
-        keys = [slice(h * HD, (h + 1) * HD) for h in range(base, base + HEAD_BATCH)]
-        values = [slice(width + h * HD, width + (h + 1) * HD) for h in range(base, base + HEAD_BATCH)]
-        scores = [dot(q_ref[:, k], kv[:, k], 1, 1) * scale for k in keys]
-        grad_probs = [dot(grads[:, k], kv[:, v], 1, 1) for k, v in zip(keys, values)]
+        pairs = range(base // 2, (base + HEAD_BATCH) // 2)
+        keys = [slice(p * 2 * HD, (p + 1) * 2 * HD) for p in pairs]
+        values = [slice(width + p * 2 * HD, width + (p + 1) * 2 * HD) for p in pairs]
+        rows_of = [slice(p * 2 * GROUP, (p + 1) * 2 * GROUP) for p in pairs]
+        scores = [dot(q_pair[r], kv[:, k], 1, 1) * scale for r, k in zip(rows_of, keys)]
+        grad_probs = [dot(g_pair[r], kv[:, v], 1, 1) for r, v in zip(rows_of, values)]
         if base + HEAD_BATCH < heads:
             project(base + HEAD_BATCH)
         raised = [jnp.exp(s - jnp.max(s, axis=-1, keepdims=True)) for s in scores]
@@ -130,9 +152,19 @@
             (p * (gp - jnp.sum(p * gp, axis=-1, keepdims=True))).astype(BF16)
             for p, gp in zip(probs, grad_probs)
         ]
-        for k, v, half, sg in zip(keys, values, halves, score_grads):
-            att_ref[:, k] = jnp.where(live, dot(half, kv[:, v], 1, 0), 0.0).astype(BF16)
-            qg_ref[:, k] = (dot(sg, kv[:, k], 1, 0) * scale).astype(BF16)
+        for p, k, v, half, sg in zip(pairs, keys, values, halves, score_grads):
+            attended = dot(half, kv[:, v], 1, 0)
+            query_grad = dot(sg, kv[:, k], 1, 0)
+            for i in range(2):
+                c = slice((2 * p + i) * HD, (2 * p + i + 1) * HD)
+                at = slice(i * GROUP, (i + 1) * GROUP), slice(i * HD, (i + 1) * HD)
+                att_ref[:, c] = jnp.where(live, attended[at], 0.0).astype(BF16)
+                qg_ref[:, c] = (query_grad[at] * scale).astype(BF16)
+        for i in range(0, len(pairs), 2):
+            k = slice(keys[i].start, keys[i + 1].stop)
+            v = slice(values[i].start, values[i + 1].stop)
+            sg = jnp.concatenate(score_grads[i : i + 2], axis=0)
+            half = jnp.concatenate(halves[i : i + 2], axis=0)
             kv_grad[k, :] = (dot(q_turned[k, :], sg, 1, 0) * scale).astype(BF16)
             kv_grad[v, :] = dot(g_turned[k, :], half, 1, 0).astype(BF16)
     terms = jnp.transpose(dot(w_ref[...], kv_grad[...], 1, 0)).astype(BF16)
@@ -174,8 +206,10 @@
             scratch_shapes=[
                 pltpu.VMEM((keys, 2 * width), BF16),
                 pltpu.VMEM((2 * width, keys), BF16),
-                pltpu.VMEM((width, GROUP), BF16),
-                pltpu.VMEM((width, GROUP), BF16),
+                pltpu.VMEM((width // 2, 2 * HD), BF16),
+                pltpu.VMEM((width // 2, 2 * HD), BF16),
+                pltpu.VMEM((width, 4 * GROUP), BF16),
+                pltpu.VMEM((width, 4 * GROUP), BF16),
             ],
         ),
         input_output_aliases={5 + n: n for n in range(len(before))},
@@ -200,10 +234,10 @@
     held, row_tokens, enc = database.shape
     width = queries.shape[2]
     chunk_groups = group_count // CHUNKS
-    own_tokens = row_tokens // line
+    own_tokens = row_tokens // (2 * line)
 
     core = lax.axis_index("c").astype(jnp.int32).reshape(1)
-    own = exchange(spread(core, neighbours.reshape(ref_count), database, seq_count), SEQ)
+    own = exchange(spread(core, neighbours[0].T, database, seq_count), SEQ)
     other = lax.ppermute(own, "c", [(0, 1), (1, 0)])
     id_tile = held // 2 * (enc // LANES)
     all_ids = own[:, id_tile, 0, :ref_count].astype(jnp.int32).reshape(-1)
@@ -225,15 +259,15 @@
     )
     column = jnp.where(column_live, column, -1)
     column, _ = lax.optimization_barrier((column, packed[-1]))
-    line_ids = lax.all_gather(column, DP, axis=0, tiled=False).reshape(line, group_count, 2)
+    line_ids = lax.all_gather(column, "y", axis=0, tiled=False).reshape(line, group_count, 1, 2, 1)
+    slots = seq_count * held * own_tokens
+    other_core = (jnp.arange(2) != core)[None, None, :, None, None]
     keys = jnp.where(
-        line_ids[..., None] >= 0, line_ids[..., None] * own_tokens + jnp.arange(own_tokens), -1
+        line_ids >= 0, other_core * slots + line_ids * own_tokens + jnp.arange(own_tokens), -1
     )
-
-    slots = seq_count * held * own_tokens
     matches = [
         (
-            jnp.arange(slots)[:, None]
+            jnp.arange(2 * slots)[:, None]
             == keys[:, c * chunk_groups : (c + 1) * chunk_groups].reshape(1, -1)
         ).astype(BF16)
         for c in range(CHUNKS)
@@ -241,13 +275,15 @@
     live, matches = lax.optimization_barrier((live, matches))
 
     done = ()
-    total = jnp.zeros((slots, enc), F32)
+    total = jnp.zeros((2 * slots, enc), F32)
     for c in range(CHUNKS):
         *done, terms = attend(
             live, rows[c], kv_weight, queries[0], out_grad[0], done, c * chunk_groups, line
         )
         back = exchange(terms, LINE)
         total = total + jnp.dot(matches[c], back.reshape(-1, enc), preferred_element_type=F32)
+    given = lax.ppermute(total[slots:].astype(BF16), "c", [(0, 1), (1, 0)])
+    total = total[:slots] + given
     owned = exchange(total.astype(BF16).reshape(seq_count, held * own_tokens, enc), SEQ)
     owned = owned.reshape(x_count, z_count, held, own_tokens, enc).astype(F32).sum(axis=1)
     row_grad = owned.transpose(1, 0, 2, 3).reshape(held, x_count * own_tokens, enc)

time: 161 us -> 161 us (level)
  blocking collectives: 47.4 us -> 26.5 us
  waiting for transfers between devices: 27.1 us -> 38.2 us
  starting transfers between devices: 23.1 us -> 30.7 us
  matrix products: 3.28 us -> 5.85 us
    all_to_all x2 -> x1, blocking collectives: 35.3 us -> 15.3 us  [exchange(): return lax.all_to_all(block, axes, split_axis=0, concat_axis=0, tiled=True)]
    all_to_all x4 -> x5, waiting for transfers between devices: 25.4 us -> 34.9 us  [exchange(): return lax.all_to_all(block, axes, split_axis=0, concat_axis=0, tiled=True)]
    all_to_all x4 -> x5, starting transfers between devices: 23.1 us -> 30.6 us  [exchange(): return lax.all_to_all(block, axes, split_axis=0, concat_axis=0, tiled=True)]
    dot_general x2, matrix products: 3.28 us -> 5.85 us  [body(): jnp.dot(matches[c], back.reshape(-1, enc), preferred_element_type=F32)]
    ppermute x0 -> x1, waiting for transfers between devices: none -> 1.8 us  [body(): given = lax.ppermute(total[slots:].astype(BF16), 'c', [(0, 1), (1, 0)])]
  transfers between devices with their start and end apart: 5 -> 7, of which waited for: 3 -> 5; matrix products, arithmetic and copies ran while one was open for 2% -> 4% of each run, Pallas kernels for 31% -> 30%
where the time goes in v3:
time: 161 us; the launch traced here: 160 us
  Pallas kernels  53.6 us (33%)
  waiting for transfers between devices  38.2 us (24%)
  starting transfers between devices  30.7 us (19%)
  blocking collectives  26.5 us (16%)
  matrix products  5.85 us (4%)
  other arithmetic  2.52 us (2%)
  local copies, waits for them, and re-layouts  1.73 us (1%)
    pallas_call x2, Pallas kernels, attend(): pl.pallas_call(functools.partial(attend_kernel, width // HD, first_group)...  46.3 us
    all_to_all x5, waiting for transfers between devices, exchange(): return lax.all_to_all(block, axes, split_axis=0, concat_axis=0, tiled=True)  34.9 us
    all_to_all x5, starting transfers between devices, exchange(): return lax.all_to_all(block, axes, split_axis=0, concat_axis=0, tiled=True)  30.6 us
    all_to_all x1, blocking collectives, exchange(): return lax.all_to_all(block, axes, split_axis=0, concat_axis=0, tiled=True)  15.3 us
    all_gather x1, blocking collectives, body(): lax.all_gather(column, 'y', axis=0, tiled=False)  11.2 us
    dot_general x2, matrix products, body(): jnp.dot(matches[c], back.reshape(-1, enc), preferred_element_type=F32)  5.85 us
    pallas_call x2, Pallas kernels, pack(): pl.pallas_call(functools.partial(pack_kernel, first_group, group_count, c...  4.77 us
  transfers between devices with their start and end apart: 7, of which 5 were waited for; matrix products, arithmetic and copies ran while one was open for 4% of the time, Pallas kernels for 30%

profile of v3, /device:TPU:0, one launch (start us, length us, event | category | flops | bytes accessed | tf_op | source)
XLA Modules:
  0.0 160.0 jit_solution(7126166204014456522)
XLA Ops:
  0.6 2.6 %spread.1 = bf16[16,15,8,128]{3,2,1,0:T(8,128)(2,1)} custom-call(s32[1]{0:T(128)} %bitcast.1.core_ref, s32[2,6]{1,0:T(2,128)} %bitcast.29, bf16[4,128,896]{2,1,0:T(8,128)(2,1)} %rows_ref.1), custom_call_target="tpu_custom_call" | custom-call | tf_op jit(solution)/shard_map/spread/pallas_call | solution.py:53
  3.3 8.0 %all-to-all-start = ((bf16[16,15,8,128]{3,2,1,0:T(8,128)(2,1)}), bf16[16,15,8,128]{3,2,1,0:T(8,128)(2,1)S(1)}, u32[]{:S(2)}, u32[]{:S(2)}) async-start(bf16[16,15,8,128]{3,2,1,0:T(8,128)(2,1)} %spread.1), calls=%async_computation | async-start | bytes 983040 | tf_op jit(solution)/shard_map/all_to_all | solution.py:223
  11.2 11.1 %all-to-all-done.own_ref = bf16[16,15,8,128]{3,2,1,0:T(8,128)(2,1)S(1)} async-done(((bf16[16,15,8,128]{3,2,1,0:T(8,128)(2,1)}), bf16[16,15,8,128]{3,2,1,0:T(8,128)(2,1)S(1)}, u32[]{:S(2)}, u32[]{:S(2)}) %all-to-all-start) | async-done | bytes 491552 | tf_op jit(solution)/shard_map/all_to_all | solution.py:223
  22.7 1.5 collective-permute-done.other_ref
  24.2 2.4 %pack.3 = bf16[16,3,16,896]{3,2,1,0:T(8,128)(2,1)} custom-call(s32[1]{0:T(128)} %bitcast.1.core_ref, s32[192]{0:T(256)S(1)} %pad_add_fusion.ids_ref, bf16[16,15,8,128]{3,2,1,0:T(8,128)(2,1)S(1)} %all-to-all-done.own_ref, bf16[16,15,8,128]{3,2,1,0:T(8,128)(2,1)S(1)} %collective-permute-done.other_ref), custom_call_target="tpu_custom_call" | custom-call | tf_op jit(solution)/shard_map/pack/pallas_call | solution.py:91
  26.6 3.7 %all-to-all-start.2 = ((bf16[16,3,16,896]{3,2,1,0:T(8,128)(2,1)}), bf16[16,3,16,896]{3,2,1,0:T(8,128)(2,1)S(1)}, u32[]{:S(2)}, u32[]{:S(2)}) async-start(bf16[16,3,16,896]{3,2,1,0:T(8,128)(2,1)} %pack.3), calls=%async_computation.2 | async-start | bytes 2752512 | tf_op jit(solution)/shard_map/all_to_all | solution.py:223
  30.4 2.4 %pack.2 = bf16[16,3,16,896]{3,2,1,0:T(8,128)(2,1)} custom-call(s32[1]{0:T(128)} %bitcast.1.core_ref, s32[192]{0:T(256)S(1)} %pad_add_fusion.ids_ref, bf16[16,15,8,128]{3,2,1,0:T(8,128)(2,1)S(1)} %all-to-all-done.own_ref, bf16[16,15,8,128]{3,2,1,0:T(8,128)(2,1)S(1)} %collective-permute-done.other_ref), custom_call_target="tpu_custom_call" | custom-call | tf_op jit(solution)/shard_map/pack/pallas_call | solution.py:91
  32.8 11.2 %all-gather.1 = s32[4,4,12]{2,1,0:T(4,128)S(1)} all-gather(s32[1,4,12]{2,1,0:T(4,128)S(1)} %bitcast.26), channel_id=2, replica_groups=mesh['y'=4,'c'=2,'x'=4,'z'=4] {'y'}, dimensions={0}, use_global_device_ids=true | all-gather | bytes 960 | tf_op jit(solution)/shard_map/all_gather | solution.py:262
  44.3 0.5 add_select_fusion
  45.1 7.5 %all-to-all-done.2.rows_ref = bf16[16,3,16,896]{3,2,1,0:T(8,128)(2,1)S(1)} async-done(((bf16[16,3,16,896]{3,2,1,0:T(8,128)(2,1)}), bf16[16,3,16,896]{3,2,1,0:T(8,128)(2,1)S(1)}, u32[]{:S(2)}, u32[]{:S(2)}) %all-to-all-start.2) | async-done | bytes 1376288 | tf_op jit(solution)/shard_map/all_to_all | solution.py:223
  52.6 4.4 %all-to-all-start.1 = ((bf16[16,3,16,896]{3,2,1,0:T(8,128)(2,1)}), bf16[16,3,16,896]{3,2,1,0:T(8,128)(2,1)}, u32[]{:S(2)}, u32[]{:S(2)}) async-start(bf16[16,3,16,896]{3,2,1,0:T(8,128)(2,1)} %pack.2), calls=%async_computation.1 | async-start | bytes 2752512 | tf_op jit(solution)/shard_map/all_to_all | solution.py:223
  57.1 1.4 fusion
  58.5 22.9 %attend.2 = (bf16[384,2048]{1,0:T(8,128)(2,1)}, bf16[384,2048]{1,0:T(8,128)(2,1)}, bf16[16,3,16,896]{3,2,1,0:T(8,128)(2,1)}) custom-call(s32[1]{0:T(128)} %bitcast.live_ref, bf16[16,3,16,896]{3,2,1,0:T(8,128)(2,1)S(1)} %all-to-all-done.2.rows_ref, bf16[896,4096]{1,0:T(8,128)(2,1)} %w_ref.3, bf16[384,2048]{1,0:T(8,128)(2,1)} %bitcast.30, ...), custom_call_target="tpu_custom_call" | custom-call | flops 12482248704 | bytes 16777216 | tf_op jit(solution)/shard_map/attend/pallas_call | solution.py:184
  81.3 7.3 %all-to-all-start.3 = ((bf16[16,3,16,896]{3,2,1,0:T(8,128)(2,1)}), bf16[16,3,16,896]{3,2,1,0:T(8,128)(2,1)S(1)}, u32[]{:S(2)}, u32[]{:S(2)}) async-start(bf16[16,3,16,896]{3,2,1,0:T(8,128)(2,1)} %get-tuple-element.20), calls=%async_computation.3 | async-start | bytes 2752512 | tf_op jit(solution)/shard_map/all_to_all | solution.py:223
  88.7 23.4 %attend.3 = (bf16[384,2048]{1,0:T(8,128)(2,1)}, bf16[384,2048]{1,0:T(8,128)(2,1)}, bf16[16,3,16,896]{3,2,1,0:T(8,128)(2,1)}) custom-call(s32[1]{0:T(128)} %bitcast.live_ref, bf16[16,3,16,896]{3,2,1,0:T(8,128)(2,1)} %all-to-all-done.1.rows_ref, bf16[896,4096]{1,0:T(8,128)(2,1)} %w_ref.3, ...), custom_call_target="tpu_custom_call", output_to_operand_aliasing={{0}: (5, {}), {1}: (6, {})} | custom-call | flops 12482248704 | bytes 16777216 | tf_op jit(solution)/shard_map/attend/pallas_call | solution.py:184
  112.1 7.2 %all-to-all-start.4 = ((bf16[16,3,16,896]{3,2,1,0:T(8,128)(2,1)}), bf16[16,3,16,896]{3,2,1,0:T(8,128)(2,1)S(1)}, u32[]{:S(2)}, u32[]{:S(2)}) async-start(bf16[16,3,16,896]{3,2,1,0:T(8,128)(2,1)} %get-tuple-element.22), calls=%async_computation.4 | async-start | bytes 2752512 | tf_op jit(solution)/shard_map/all_to_all | solution.py:223
  119.3 3.4 %fusion.5 = f32[512,896]{1,0:T(8,128)} fusion(bf16[512,768]{1,0:T(8,128)(2,1)} %get-tuple-element.19, bf16[768,896]{1,0:T(8,128)(2,1)S(1)} %bitcast.23), kind=kOutput, calls=%fused_computation.21 | convolution fusion | flops 704643072 | bytes 3997696 | tf_op jit(solution)/shard_map/dot_general | solution.py:284
  122.7 16.3 %all-to-all-done.4 = bf16[16,3,16,896]{3,2,1,0:T(8,128)(2,1)S(1)} async-done(((bf16[16,3,16,896]{3,2,1,0:T(8,128)(2,1)}), bf16[16,3,16,896]{3,2,1,0:T(8,128)(2,1)S(1)}, u32[]{:S(2)}, u32[]{:S(2)}) %all-to-all-start.4) | async-done | bytes 1376288 | tf_op jit(solution)/shard_map/all_to_all | solution.py:223
  138.9 2.5 %convolution_add_fusion = f32[512,896]{1,0:T(8,128)S(1)} fusion(f32[512,896]{1,0:T(8,128)} %fusion.5, bf16[512,768]{1,0:T(8,128)(2,1)S(1)} %get-tuple-element.21, bf16[768,896]{1,0:T(8,128)(2,1)S(1)} %bitcast.21), kind=kOutput, calls=%fused_computation.4 | convolution fusion | flops 705101824 | bytes 5832704 | tf_op jit(solution)/shard_map/dot_general | solution.py:284
  141.5 1.8 %collective-permute-done.1 = bf16[256,896]{1,0:T(8,128)(2,1)S(1)} collective-permute-done((bf16[256,896]{1,0:T(8,128)(2,1)S(1)}, bf16[256,896]{1,0:T(8,128)(2,1)S(1)}, u32[]{:S(2)}, u32[]{:S(2)}) %collective-permute-start.1) | collective-permute-done | bytes 458784 | tf_op jit(solution)/shard_map/ppermute | solution.py:285
  143.5 15.3 %all_to_all.30 = bf16[16,16,896]{2,1,0:T(8,128)(2,1)S(1)} all-to-all(bf16[16,16,896]{2,1,0:T(8,128)(2,1)S(1)} %bitcast.22), channel_id=1, replica_groups=mesh['y'=4,'c'=2,'x'=4,'z'=4] {'x','z'}, dimensions={0} | all-to-all | bytes 917504 | tf_op jit(solution)/shard_map/all_to_all | solution.py:223
  158.7 0.2 reshape.96
  159.0 0.2 reduce_sum.9
  159.3 0.7 copy.23
  (25 shorter events, 1.3 us)
Async XLA Ops:
  3.3 19.1 %all-to-all-start = ((bf16[16,15,8,128]{3,2,1,0:T(8,128)(2,1)}), bf16[16,15,8,128]{3,2,1,0:T(8,128)(2,1)S(1)}, u32[]{:S(2)}, u32[]{:S(2)}) async-start(bf16[16,15,8,128]{3,2,1,0:T(8,128)(2,1)} %spread.1), calls=%async_computation | async-start | bytes 983040 | tf_op jit(solution)/shard_map/all_to_all | solution.py:223
  22.4 1.9 %collective-permute-start = (bf16[16,15,8,128]{3,2,1,0:T(8,128)(2,1)S(1)}, bf16[16,15,8,128]{3,2,1,0:T(8,128)(2,1)S(1)}, u32[]{:S(2)}, u32[]{:S(2)}) collective-permute-start(bf16[16,15,8,128]{3,2,1,0:T(8,128)(2,1)S(1)} %all-to-all-done.own_ref), channel_id=1, source_target_pairs={{0,16},{16,0},{1,17},{17,1},{2,18},{18,2},{3,19},{19,3},{4,20},{20... | collective-permute-start | bytes 1474568 | tf_op jit(solution)/shard_map/ppermute | solution.py:241
  26.6 26.0 %all-to-all-start.2 = ((bf16[16,3,16,896]{3,2,1,0:T(8,128)(2,1)}), bf16[16,3,16,896]{3,2,1,0:T(8,128)(2,1)S(1)}, u32[]{:S(2)}, u32[]{:S(2)}) async-start(bf16[16,3,16,896]{3,2,1,0:T(8,128)(2,1)} %pack.3), calls=%async_computation.2 | async-start | bytes 2752512 | tf_op jit(solution)/shard_map/all_to_all | solution.py:223
  52.6 28.7 %all-to-all-start.1 = ((bf16[16,3,16,896]{3,2,1,0:T(8,128)(2,1)}), bf16[16,3,16,896]{3,2,1,0:T(8,128)(2,1)}, u32[]{:S(2)}, u32[]{:S(2)}) async-start(bf16[16,3,16,896]{3,2,1,0:T(8,128)(2,1)} %pack.2), calls=%async_computation.1 | async-start | bytes 2752512 | tf_op jit(solution)/shard_map/all_to_all | solution.py:223
  81.3 30.7 %all-to-all-start.3 = ((bf16[16,3,16,896]{3,2,1,0:T(8,128)(2,1)}), bf16[16,3,16,896]{3,2,1,0:T(8,128)(2,1)S(1)}, u32[]{:S(2)}, u32[]{:S(2)}) async-start(bf16[16,3,16,896]{3,2,1,0:T(8,128)(2,1)} %get-tuple-element.20), calls=%async_computation.3 | async-start | bytes 2752512 | tf_op jit(solution)/shard_map/all_to_all | solution.py:223
  112.1 26.9 %all-to-all-start.4 = ((bf16[16,3,16,896]{3,2,1,0:T(8,128)(2,1)}), bf16[16,3,16,896]{3,2,1,0:T(8,128)(2,1)S(1)}, u32[]{:S(2)}, u32[]{:S(2)}) async-start(bf16[16,3,16,896]{3,2,1,0:T(8,128)(2,1)} %get-tuple-element.22), calls=%async_computation.4 | async-start | bytes 2752512 | tf_op jit(solution)/shard_map/all_to_all | solution.py:223
  141.5 1.9 %collective-permute-start.1 = (bf16[256,896]{1,0:T(8,128)(2,1)S(1)}, bf16[256,896]{1,0:T(8,128)(2,1)S(1)}, u32[]{:S(2)}, u32[]{:S(2)}) collective-permute-start(bf16[256,896]{1,0:T(8,128)(2,1)S(1)} %slice.41), channel_id=1, source_target_pairs={{0,16},{16,0},{1,17},{17,1},{2,18},{18,2},{3,19},{19,3},{4,20},{20... | collective-permute-start | bytes 1376264 | tf_op jit(solution)/shard_map/ppermute | solution.py:285

commit v4 on v3

--- a/solution.py
+++ b/solution.py
@@ -12,7 +12,7 @@
 GROUP = 64
 SEQ = ("x", "z")
 DP = ("y", "c")
-LINE = ("y", "x")
+LINE = ("y", "c", "x")
 CHUNKS = 2
 HEAD_BATCH = 8
 LANES = 128
@@ -33,17 +33,14 @@
         for r in range(2):
             ids = jnp.where(lanes == 2 * g + r, ids_ref[r, g], ids)
     ids = ids.astype(F32).astype(BF16)
-    for y in range(tokens // 32):
+    for pair in range(tokens // 16):
         for j in range(half):
             for t in range(lane_tiles):
-                lane = slice(t * LANES, (t + 1) * LANES)
-                a = rows_ref[j, 32 * y : 32 * y + 16, lane].astype(F32)
-                b = rows_ref[j, 32 * y + 16 : 32 * y + 32, lane].astype(F32)
-                for x in range(4):
-                    piece = jnp.concatenate([a[4 * x : 4 * x + 4], b[4 * x : 4 * x + 4]], axis=0)
-                    out_ref[4 * y + x, j * lane_tiles + t] = piece.astype(BF16)
-    for dest in range(out_ref.shape[0]):
-        out_ref[dest, half * lane_tiles] = ids
+                rows = rows_ref[j, 16 * pair : 16 * pair + 16, t * LANES : (t + 1) * LANES].astype(F32)
+                out_ref[2 * pair, j * lane_tiles + t] = rows[:8].astype(BF16)
+                out_ref[2 * pair + 1, j * lane_tiles + t] = rows[8:].astype(BF16)
+        out_ref[2 * pair, half * lane_tiles] = ids
+        out_ref[2 * pair + 1, half * lane_tiles] = ids
 
 
 def spread(core, ids, database, dests):
@@ -234,7 +231,7 @@
     held, row_tokens, enc = database.shape
     width = queries.shape[2]
     chunk_groups = group_count // CHUNKS
-    own_tokens = row_tokens // (2 * line)
+    own_tokens = row_tokens // line
 
     core = lax.axis_index("c").astype(jnp.int32).reshape(1)
     own = exchange(spread(core, neighbours[0].T, database, seq_count), SEQ)
@@ -259,15 +256,15 @@
     )
     column = jnp.where(column_live, column, -1)
     column, _ = lax.optimization_barrier((column, packed[-1]))
-    line_ids = lax.all_gather(column, "y", axis=0, tiled=False).reshape(line, group_count, 1, 2, 1)
+    line_ids = lax.all_gather(column, DP, axis=0, tiled=False).reshape(line, group_count, 2)
+    keys = jnp.where(
+        line_ids[..., None] >= 0, line_ids[..., None] * own_tokens + jnp.arange(own_tokens), -1
+    )
+
     slots = seq_count * held * own_tokens
-    other_core = (jnp.arange(2) != core)[None, None, :, None, None]
-    keys = jnp.where(
-        line_ids >= 0, other_core * slots + line_ids * own_tokens + jnp.arange(own_tokens), -1
-    )
     matches = [
         (
-            jnp.arange(2 * slots)[:, None]
+            jnp.arange(slots)[:, None]
             == keys[:, c * chunk_groups : (c + 1) * chunk_groups].reshape(1, -1)
         ).astype(BF16)
         for c in range(CHUNKS)
@@ -275,15 +272,13 @@
     live, matches = lax.optimization_barrier((live, matches))
 
     done = ()
-    total = jnp.zeros((2 * slots, enc), F32)
+    total = jnp.zeros((slots, enc), F32)
     for c in range(CHUNKS):
         *done, terms = attend(
             live, rows[c], kv_weight, queries[0], out_grad[0], done, c * chunk_groups, line
         )
         back = exchange(terms, LINE)
         total = total + jnp.dot(matches[c], back.reshape(-1, enc), preferred_element_type=F32)
-    given = lax.ppermute(total[slots:].astype(BF16), "c", [(0, 1), (1, 0)])
-    total = total[:slots] + given
     owned = exchange(total.astype(BF16).reshape(seq_count, held * own_tokens, enc), SEQ)
     owned = owned.reshape(x_count, z_count, held, own_tokens, enc).astype(F32).sum(axis=1)
     row_grad = owned.transpose(1, 0, 2, 3).reshape(held, x_count * own_tokens, enc)

time: 161 us -> 159 us (0.988)
  blocking collectives: 26.5 us -> 47.4 us
  waiting for transfers between devices: 38.2 us -> 27.1 us
  starting transfers between devices: 30.7 us -> 23.1 us
  matrix products: 5.85 us -> 3.28 us
    all_to_all x1 -> x2, blocking collectives: 15.3 us -> 35.3 us  [exchange(): return lax.all_to_all(block, axes, split_axis=0, concat_axis=0, tiled=True)]
    all_to_all x5 -> x4, waiting for transfers between devices: 34.9 us -> 25.4 us  [exchange(): return lax.all_to_all(block, axes, split_axis=0, concat_axis=0, tiled=True)]
    all_to_all x5 -> x4, starting transfers between devices: 30.6 us -> 23.1 us  [exchange(): return lax.all_to_all(block, axes, split_axis=0, concat_axis=0, tiled=True)]
    dot_general x2, matrix products: 5.85 us -> 3.28 us  [body(): jnp.dot(matches[c], back.reshape(-1, enc), preferred_element_type=F32)]
    ppermute x1 -> x0, waiting for transfers between devices: 1.8 us -> none  [body(): given = lax.ppermute(total[slots:].astype(BF16), 'c', [(0, 1), (1, 0)])]
  transfers between devices with their start and end apart: 7 -> 5, of which waited for: 5 -> 3; matrix products, arithmetic and copies ran while one was open for 4% -> 2% of each run, Pallas kernels for 30% -> 31%
where the time goes in v4:
time: 159 us; the launch traced here: 158 us
  Pallas kernels  53.6 us (34%)
  blocking collectives  47.4 us (30%)
  waiting for transfers between devices  27.1 us (17%)
  starting transfers between devices  23.1 us (15%)
  matrix products  3.28 us (2%)
  local copies, waits for them, and re-layouts  1.74 us (1%)
    pallas_call x2, Pallas kernels, attend(): pl.pallas_call(functools.partial(attend_kernel, width // HD, first_group)...  46.3 us
    all_to_all x2, blocking collectives, exchange(): return lax.all_to_all(block, axes, split_axis=0, concat_axis=0, tiled=True)  35.3 us
    all_to_all x4, waiting for transfers between devices, exchange(): return lax.all_to_all(block, axes, split_axis=0, concat_axis=0, tiled=True)  25.4 us
    all_to_all x4, starting transfers between devices, exchange(): return lax.all_to_all(block, axes, split_axis=0, concat_axis=0, tiled=True)  23.1 us
    all_gather x1, blocking collectives, body(): lax.all_gather(column, DP, axis=0, tiled=False)  12.1 us
    pallas_call x2, Pallas kernels, pack(): pl.pallas_call(functools.partial(pack_kernel, first_group, group_count, c...  4.77 us
    dot_general x2, matrix products, body(): jnp.dot(matches[c], back.reshape(-1, enc), preferred_element_type=F32)  3.28 us
  transfers between devices with their start and end apart: 5, of which 3 were waited for; matrix products, arithmetic and copies ran while one was open for 2% of the time, Pallas kernels for 31%

profile of v4, /device:TPU:0, one launch (start us, length us, event | category | flops | bytes accessed | tf_op | source)
XLA Modules:
  0.0 158.2 jit_solution(8616549494586700816)
XLA Ops:
  0.6 2.6 %spread.1 = bf16[16,15,8,128]{3,2,1,0:T(8,128)(2,1)} custom-call(s32[1]{0:T(128)} %bitcast.1.core_ref, s32[2,6]{1,0:T(2,128)} %bitcast.29, bf16[4,128,896]{2,1,0:T(8,128)(2,1)} %rows_ref.1), custom_call_target="tpu_custom_call" | custom-call | tf_op jit(solution)/shard_map/spread/pallas_call | solution.py:50
  3.2 19.1 %all_to_all.30.own_ref = bf16[16,15,8,128]{3,2,1,0:T(8,128)(2,1)S(1)} all-to-all(bf16[16,15,8,128]{3,2,1,0:T(8,128)(2,1)} %spread.1), channel_id=1, replica_groups=mesh['y'=4,'c'=2,'x'=4,'z'=4] {'x','z'}, dimensions={0} | all-to-all | bytes 983040 | tf_op jit(solution)/shard_map/all_to_all | solution.py:220
  22.5 1.6 %collective-permute-done.other_ref = bf16[16,15,8,128]{3,2,1,0:T(8,128)(2,1)S(1)} collective-permute-done((bf16[16,15,8,128]{3,2,1,0:T(8,128)(2,1)S(1)}, bf16[16,15,8,128]{3,2,1,0:T(8,128)(2,1)S(1)}, u32[]{:S(2)}, u32[]{:S(2)}) %collective-permute-start) | collective-permute-done | bytes 491552 | tf_op jit(solution)/shard_map/ppermute | solution.py:238
  24.2 2.4 %pack.3 = bf16[16,3,16,896]{3,2,1,0:T(8,128)(2,1)} custom-call(s32[1]{0:T(128)} %bitcast.1.core_ref, s32[192]{0:T(256)S(1)} %pad_add_fusion.ids_ref, bf16[16,15,8,128]{3,2,1,0:T(8,128)(2,1)S(1)} %all_to_all.30.own_ref, bf16[16,15,8,128]{3,2,1,0:T(8,128)(2,1)S(1)} %collective-permute-done.other_ref), custom_call_target="tpu_custom_call" | custom-call | tf_op jit(solution)/shard_map/pack/pallas_call | solution.py:88
  26.5 3.7 %all-to-all-start.2 = ((bf16[16,3,16,896]{3,2,1,0:T(8,128)(2,1)}), bf16[16,3,16,896]{3,2,1,0:T(8,128)(2,1)S(1)}, u32[]{:S(2)}, u32[]{:S(2)}) async-start(bf16[16,3,16,896]{3,2,1,0:T(8,128)(2,1)} %pack.3), calls=%async_computation.2 | async-start | bytes 2752512 | tf_op jit(solution)/shard_map/all_to_all | solution.py:220
  30.5 2.4 %pack.2 = bf16[16,3,16,896]{3,2,1,0:T(8,128)(2,1)} custom-call(s32[1]{0:T(128)} %bitcast.1.core_ref, s32[192]{0:T(256)S(1)} %pad_add_fusion.ids_ref, bf16[16,15,8,128]{3,2,1,0:T(8,128)(2,1)S(1)} %all_to_all.30.own_ref, bf16[16,15,8,128]{3,2,1,0:T(8,128)(2,1)S(1)} %collective-permute-done.other_ref), custom_call_target="tpu_custom_call" | custom-call | tf_op jit(solution)/shard_map/pack/pallas_call | solution.py:88
  32.9 12.1 %all-gather.1 = s32[8,4,12]{2,1,0:T(4,128)S(1)} all-gather(s32[1,4,12]{2,1,0:T(4,128)S(1)} %bitcast.26), channel_id=2, replica_groups=mesh['y'=4,'c'=2,'x'=4,'z'=4] {'y','c'}, dimensions={0}, use_global_device_ids=true | all-gather | bytes 1728 | tf_op jit(solution)/shard_map/all_gather | solution.py:259
  45.2 0.6 add_select_fusion
  45.8 0.2 eq.31
  46.0 0.2 eq.35
  46.1 6.4 %all-to-all-done.2.rows_ref = bf16[16,3,16,896]{3,2,1,0:T(8,128)(2,1)S(1)} async-done(((bf16[16,3,16,896]{3,2,1,0:T(8,128)(2,1)}), bf16[16,3,16,896]{3,2,1,0:T(8,128)(2,1)S(1)}, u32[]{:S(2)}, u32[]{:S(2)}) %all-to-all-start.2) | async-done | bytes 1376288 | tf_op jit(solution)/shard_map/all_to_all | solution.py:220
  52.6 4.4 %all-to-all-start.1 = ((bf16[16,3,16,896]{3,2,1,0:T(8,128)(2,1)}), bf16[16,3,16,896]{3,2,1,0:T(8,128)(2,1)}, u32[]{:S(2)}, u32[]{:S(2)}) async-start(bf16[16,3,16,896]{3,2,1,0:T(8,128)(2,1)} %pack.2), calls=%async_computation.1 | async-start | bytes 2752512 | tf_op jit(solution)/shard_map/all_to_all | solution.py:220
  57.0 0.2 fusion.1
  57.2 22.9 %attend.2 = (bf16[384,2048]{1,0:T(8,128)(2,1)}, bf16[384,2048]{1,0:T(8,128)(2,1)}, bf16[32,3,8,896]{3,2,1,0:T(8,128)(2,1)}) custom-call(s32[1]{0:T(128)} %bitcast.live_ref, bf16[16,3,16,896]{3,2,1,0:T(8,128)(2,1)S(1)} %all-to-all-done.2.rows_ref, bf16[896,4096]{1,0:T(8,128)(2,1)} %w_ref.3, bf16[384,2048]{1,0:T(8,128)(2,1)} %bitcast.30, ...), custom_call_target="tpu_custom_call" | custom-call | flops 12482248704 | bytes 16777216 | tf_op jit(solution)/shard_map/attend/pallas_call | solution.py:181
  80.1 7.8 %all-to-all-start.3 = ((bf16[32,3,8,896]{3,2,1,0:T(8,128)(2,1)}), bf16[32,3,8,896]{3,2,1,0:T(8,128)(2,1)S(1)}, u32[]{:S(2)}, u32[]{:S(2)}) async-start(bf16[32,3,8,896]{3,2,1,0:T(8,128)(2,1)} %get-tuple-element.20), calls=%async_computation.3 | async-start | bytes 2752512 | tf_op jit(solution)/shard_map/all_to_all | solution.py:220
  87.9 23.4 %attend.3 = (bf16[384,2048]{1,0:T(8,128)(2,1)}, bf16[384,2048]{1,0:T(8,128)(2,1)}, bf16[32,3,8,896]{3,2,1,0:T(8,128)(2,1)}) custom-call(s32[1]{0:T(128)} %bitcast.live_ref, bf16[16,3,16,896]{3,2,1,0:T(8,128)(2,1)} %all-to-all-done.1.rows_ref, bf16[896,4096]{1,0:T(8,128)(2,1)} %w_ref.3, ...), custom_call_target="tpu_custom_call", output_to_operand_aliasing={{0}: (5, {}), {1}: (6, {})} | custom-call | flops 12482248704 | bytes 16777216 | tf_op jit(solution)/shard_map/attend/pallas_call | solution.py:181
  111.3 7.2 %all-to-all-start.4 = ((bf16[32,3,8,896]{3,2,1,0:T(8,128)(2,1)}), bf16[32,3,8,896]{3,2,1,0:T(8,128)(2,1)S(1)}, u32[]{:S(2)}, u32[]{:S(2)}) async-start(bf16[32,3,8,896]{3,2,1,0:T(8,128)(2,1)} %get-tuple-element.22), calls=%async_computation.4 | async-start | bytes 2752512 | tf_op jit(solution)/shard_map/all_to_all | solution.py:220
  118.5 1.5 fusion.5
  120.0 19.0 %all-to-all-done.4 = bf16[32,3,8,896]{3,2,1,0:T(8,128)(2,1)S(1)} async-done(((bf16[32,3,8,896]{3,2,1,0:T(8,128)(2,1)}), bf16[32,3,8,896]{3,2,1,0:T(8,128)(2,1)S(1)}, u32[]{:S(2)}, u32[]{:S(2)}) %all-to-all-start.4) | async-done | bytes 1376288 | tf_op jit(solution)/shard_map/all_to_all | solution.py:220
  139.0 1.8 %fusion = bf16[256,896]{1,0:T(8,128)(2,1)S(1)} fusion(f32[256,896]{1,0:T(8,128)} %fusion.5, bf16[256,768]{1,0:T(8,128)(2,1)S(1)} %get-tuple-element.21, bf16[768,896]{1,0:T(8,128)(2,1)S(1)} %bitcast.21), kind=kOutput, calls=%fused_computation.1 | convolution fusion | flops 352780288 | bytes 3145728 | tf_op jit(solution)/shard_map/dot_general | solution.py:281
  140.7 16.2 %all_to_all.31 = bf16[16,16,896]{2,1,0:T(8,128)(2,1)S(1)} all-to-all(bf16[16,16,896]{2,1,0:T(8,128)(2,1)S(1)} %bitcast.23), channel_id=1, replica_groups=mesh['y'=4,'c'=2,'x'=4,'z'=4] {'x','z'}, dimensions={0} | all-to-all | bytes 917504 | tf_op jit(solution)/shard_map/all_to_all | solution.py:220
  156.9 0.2 reshape.82
  157.2 0.2 reduce_sum.9
  157.5 0.7 copy.31
  (20 shorter events, 0.7 us)
Async XLA Ops:
  22.3 1.9 %collective-permute-start = (bf16[16,15,8,128]{3,2,1,0:T(8,128)(2,1)S(1)}, bf16[16,15,8,128]{3,2,1,0:T(8,128)(2,1)S(1)}, u32[]{:S(2)}, u32[]{:S(2)}) collective-permute-start(bf16[16,15,8,128]{3,2,1,0:T(8,128)(2,1)S(1)} %all_to_all.30.own_ref), channel_id=1, source_target_pairs={{0,16},{16,0},{1,17},{17,1},{2,18},{18,2},{3,19},{19,3},{4,20},{20... | collective-permute-start | bytes 1474568 | tf_op jit(solution)/shard_map/ppermute | solution.py:238
  26.5 26.0 %all-to-all-start.2 = ((bf16[16,3,16,896]{3,2,1,0:T(8,128)(2,1)}), bf16[16,3,16,896]{3,2,1,0:T(8,128)(2,1)S(1)}, u32[]{:S(2)}, u32[]{:S(2)}) async-start(bf16[16,3,16,896]{3,2,1,0:T(8,128)(2,1)} %pack.3), calls=%async_computation.2 | async-start | bytes 2752512 | tf_op jit(solution)/shard_map/all_to_all | solution.py:220
  52.6 27.5 %all-to-all-start.1 = ((bf16[16,3,16,896]{3,2,1,0:T(8,128)(2,1)}), bf16[16,3,16,896]{3,2,1,0:T(8,128)(2,1)}, u32[]{:S(2)}, u32[]{:S(2)}) async-start(bf16[16,3,16,896]{3,2,1,0:T(8,128)(2,1)} %pack.2), calls=%async_computation.1 | async-start | bytes 2752512 | tf_op jit(solution)/shard_map/all_to_all | solution.py:220
  80.1 31.2 %all-to-all-start.3 = ((bf16[32,3,8,896]{3,2,1,0:T(8,128)(2,1)}), bf16[32,3,8,896]{3,2,1,0:T(8,128)(2,1)S(1)}, u32[]{:S(2)}, u32[]{:S(2)}) async-start(bf16[32,3,8,896]{3,2,1,0:T(8,128)(2,1)} %get-tuple-element.20), calls=%async_computation.3 | async-start | bytes 2752512 | tf_op jit(solution)/shard_map/all_to_all | solution.py:220
  111.3 27.7 %all-to-all-start.4 = ((bf16[32,3,8,896]{3,2,1,0:T(8,128)(2,1)}), bf16[32,3,8,896]{3,2,1,0:T(8,128)(2,1)S(1)}, u32[]{:S(2)}, u32[]{:S(2)}) async-start(bf16[32,3,8,896]{3,2,1,0:T(8,128)(2,1)} %get-tuple-element.22), calls=%async_computation.4 | async-start | bytes 2752512 | tf_op jit(solution)/shard_map/all_to_all | solution.py:220

commit v5 on v4

--- a/solution.py
+++ b/solution.py
@@ -49,7 +49,7 @@
     out = (dests, half * (enc // LANES) + 1, tokens // dests, LANES)
     return pl.pallas_call(
         spread_kernel,
-        out_shape=pltpu.HBM(out, BF16),
+        out_shape=jax.ShapeDtypeStruct(out, BF16),
         grid_spec=pltpu.PrefetchScalarGridSpec(
             num_scalar_prefetch=2,
             grid=(1,),
@@ -80,7 +80,7 @@
                 ).astype(BF16)
         return carry
 
-    lax.fori_loop(0, out_ref.shape[0], per_dest, 0)
+    lax.fori_loop(0, out_ref.shape[0], per_dest, 0, unroll=2)
 
 
 def pack(core, ids, own, other, enc, first_group, group_count, chunk_groups):
@@ -216,6 +216,32 @@
     )(live, rows, *in_hbm(weight, queries, grads, *before))
 
 
+def collect_kernel(x_count, pieces_ref, out_ref):
+    z_count = pieces_ref.shape[0] // x_count
+    held = out_ref.shape[0]
+    own = pieces_ref.shape[1] // held
+    sums = []
+    for x in range(x_count):
+        total = pieces_ref[x * z_count].astype(F32)
+        for z in range(1, z_count):
+            total = total + pieces_ref[x * z_count + z].astype(F32)
+        sums.append(total)
+    for n in range(held):
+        out_ref[n] = jnp.concatenate([t[n * own : (n + 1) * own] for t in sums], axis=0)
+
+
+def collect(pieces, x_count, held):
+    enc = pieces.shape[2]
+    return pl.pallas_call(
+        functools.partial(collect_kernel, x_count),
+        out_shape=jax.ShapeDtypeStruct((held, x_count * pieces.shape[1] // held, enc), F32),
+        in_specs=[pl.BlockSpec(memory_space=pltpu.VMEM)],
+        out_specs=pl.BlockSpec(memory_space=pltpu.VMEM),
+        compiler_params=pltpu.CompilerParams(vmem_limit_bytes=16 << 20),
+        name="collect",
+    )(pieces)
+
+
 def exchange(block, axes):
     return lax.all_to_all(block, axes, split_axis=0, concat_axis=0, tiled=True)
 
@@ -280,8 +306,7 @@
         back = exchange(terms, LINE)
         total = total + jnp.dot(matches[c], back.reshape(-1, enc), preferred_element_type=F32)
     owned = exchange(total.astype(BF16).reshape(seq_count, held * own_tokens, enc), SEQ)
-    owned = owned.reshape(x_count, z_count, held, own_tokens, enc).astype(F32).sum(axis=1)
-    row_grad = owned.transpose(1, 0, 2, 3).reshape(held, x_count * own_tokens, enc)
+    row_grad = collect(owned, x_count, held)
     return done[0][None], done[1][None], row_grad
 
 

time: 159 us -> 157 us (0.987)
  no operation moved by 1% of the time
where the time goes in v5:
time: 157 us
  Pallas kernels  53.3 us (34%)
  blocking collectives  47.2 us (30%)
  waiting for transfers between devices  27.2 us (17%)
  starting transfers between devices  23.1 us (15%)
  matrix products  3.26 us (2%)
    pallas_call x2, Pallas kernels, attend(): pl.pallas_call(functools.partial(attend_kernel, width // HD, first_group)...  46.2 us
    all_to_all x2, blocking collectives, exchange(): return lax.all_to_all(block, axes, split_axis=0, concat_axis=0, tiled=True)  35.1 us
    all_to_all x4, waiting for transfers between devices, exchange(): return lax.all_to_all(block, axes, split_axis=0, concat_axis=0, tiled=True)  25.5 us
    all_to_all x4, starting transfers between devices, exchange(): return lax.all_to_all(block, axes, split_axis=0, concat_axis=0, tiled=True)  23.1 us
    all_gather x1, blocking collectives, body(): lax.all_gather(column, DP, axis=0, tiled=False)  12.1 us
    pallas_call x2, Pallas kernels, pack(): pl.pallas_call(functools.partial(pack_kernel, first_group, group_count, c...  4.57 us
    dot_general x2, matrix products, body(): jnp.dot(matches[c], back.reshape(-1, enc), preferred_element_type=F32)  3.26 us
  transfers between devices with their start and end apart: 5, of which 3 were waited for; matrix products, arithmetic and copies ran while one was open for 2% of the time, Pallas kernels for 31%

profile of v5, /device:TPU:0, one launch (start us, length us, event | category | flops | bytes accessed | tf_op | source)
XLA Modules:
  0.0 156.6 jit_solution(1098286700966449910)
XLA Ops:
  0.6 1.8 %spread.1 = bf16[16,15,8,128]{3,2,1,0:T(8,128)(2,1)S(1)} custom-call(s32[1]{0:T(128)} %bitcast.1.core_ref, s32[2,6]{1,0:T(2,128)} %bitcast.25, bf16[4,128,896]{2,1,0:T(8,128)(2,1)} %rows_ref.1), custom_call_target="tpu_custom_call" | custom-call | tf_op jit(solution)/shard_map/spread/pallas_call | solution.py:50
  2.4 18.9 %all_to_all.30.own_ref = bf16[16,15,8,128]{3,2,1,0:T(8,128)(2,1)S(1)} all-to-all(bf16[16,15,8,128]{3,2,1,0:T(8,128)(2,1)S(1)} %spread.1), channel_id=1, replica_groups=mesh['y'=4,'c'=2,'x'=4,'z'=4] {'x','z'}, dimensions={0} | all-to-all | bytes 983040 | tf_op jit(solution)/shard_map/all_to_all | solution.py:246
  21.5 1.6 %collective-permute-done.other_ref = bf16[16,15,8,128]{3,2,1,0:T(8,128)(2,1)S(1)} collective-permute-done((bf16[16,15,8,128]{3,2,1,0:T(8,128)(2,1)S(1)}, bf16[16,15,8,128]{3,2,1,0:T(8,128)(2,1)S(1)}, u32[]{:S(2)}, u32[]{:S(2)}) %collective-permute-start) | collective-permute-done | bytes 491552 | tf_op jit(solution)/shard_map/ppermute | solution.py:264
  23.2 2.3 %pack.3 = bf16[16,3,16,896]{3,2,1,0:T(8,128)(2,1)} custom-call(s32[1]{0:T(128)} %bitcast.1.core_ref, s32[192]{0:T(256)S(1)} %pad_add_fusion.ids_ref, bf16[16,15,8,128]{3,2,1,0:T(8,128)(2,1)S(1)} %all_to_all.30.own_ref, bf16[16,15,8,128]{3,2,1,0:T(8,128)(2,1)S(1)} %collective-permute-done.other_ref), custom_call_target="tpu_custom_call" | custom-call | tf_op jit(solution)/shard_map/pack/pallas_call | solution.py:88
  25.5 3.7 %all-to-all-start.2 = ((bf16[16,3,16,896]{3,2,1,0:T(8,128)(2,1)}), bf16[16,3,16,896]{3,2,1,0:T(8,128)(2,1)S(1)}, u32[]{:S(2)}, u32[]{:S(2)}) async-start(bf16[16,3,16,896]{3,2,1,0:T(8,128)(2,1)} %pack.3), calls=%async_computation.2 | async-start | bytes 2752512 | tf_op jit(solution)/shard_map/all_to_all | solution.py:246
  29.4 2.3 %pack.2 = bf16[16,3,16,896]{3,2,1,0:T(8,128)(2,1)} custom-call(s32[1]{0:T(128)} %bitcast.1.core_ref, s32[192]{0:T(256)S(1)} %pad_add_fusion.ids_ref, bf16[16,15,8,128]{3,2,1,0:T(8,128)(2,1)S(1)} %all_to_all.30.own_ref, bf16[16,15,8,128]{3,2,1,0:T(8,128)(2,1)S(1)} %collective-permute-done.other_ref), custom_call_target="tpu_custom_call" | custom-call | tf_op jit(solution)/shard_map/pack/pallas_call | solution.py:88
  31.7 12.1 %all-gather.1 = s32[8,4,12]{2,1,0:T(4,128)S(1)} all-gather(s32[1,4,12]{2,1,0:T(4,128)S(1)} %bitcast.22), channel_id=2, replica_groups=mesh['y'=4,'c'=2,'x'=4,'z'=4] {'y','c'}, dimensions={0}, use_global_device_ids=true | all-gather | bytes 1728 | tf_op jit(solution)/shard_map/all_gather | solution.py:285
  43.8 0.1 reshape.91
  43.9 0.1 reshape.90
  44.0 0.6 add_select_fusion
  44.7 0.2 eq.31
  44.8 0.2 eq.35
  45.0 6.5 %all-to-all-done.2.rows_ref = bf16[16,3,16,896]{3,2,1,0:T(8,128)(2,1)S(1)} async-done(((bf16[16,3,16,896]{3,2,1,0:T(8,128)(2,1)}), bf16[16,3,16,896]{3,2,1,0:T(8,128)(2,1)S(1)}, u32[]{:S(2)}, u32[]{:S(2)}) %all-to-all-start.2) | async-done | bytes 1376288 | tf_op jit(solution)/shard_map/all_to_all | solution.py:246
  51.5 4.4 %all-to-all-start.1 = ((bf16[16,3,16,896]{3,2,1,0:T(8,128)(2,1)}), bf16[16,3,16,896]{3,2,1,0:T(8,128)(2,1)}, u32[]{:S(2)}, u32[]{:S(2)}) async-start(bf16[16,3,16,896]{3,2,1,0:T(8,128)(2,1)} %pack.2), calls=%async_computation.1 | async-start | bytes 2752512 | tf_op jit(solution)/shard_map/all_to_all | solution.py:246
  55.9 0.2 fusion.1
  56.1 22.9 %attend.2 = (bf16[384,2048]{1,0:T(8,128)(2,1)}, bf16[384,2048]{1,0:T(8,128)(2,1)}, bf16[32,3,8,896]{3,2,1,0:T(8,128)(2,1)}) custom-call(s32[1]{0:T(128)} %bitcast.live_ref, bf16[16,3,16,896]{3,2,1,0:T(8,128)(2,1)S(1)} %all-to-all-done.2.rows_ref, bf16[896,4096]{1,0:T(8,128)(2,1)} %w_ref.3, bf16[384,2048]{1,0:T(8,128)(2,1)} %bitcast.26, ...), custom_call_target="tpu_custom_call" | custom-call | flops 12482248704 | bytes 16777216 | tf_op jit(solution)/shard_map/attend/pallas_call | solution.py:181
  79.0 7.8 %all-to-all-start.3 = ((bf16[32,3,8,896]{3,2,1,0:T(8,128)(2,1)}), bf16[32,3,8,896]{3,2,1,0:T(8,128)(2,1)S(1)}, u32[]{:S(2)}, u32[]{:S(2)}) async-start(bf16[32,3,8,896]{3,2,1,0:T(8,128)(2,1)} %get-tuple-element.20), calls=%async_computation.3 | async-start | bytes 2752512 | tf_op jit(solution)/shard_map/all_to_all | solution.py:246
  86.8 23.3 %attend.3 = (bf16[384,2048]{1,0:T(8,128)(2,1)}, bf16[384,2048]{1,0:T(8,128)(2,1)}, bf16[32,3,8,896]{3,2,1,0:T(8,128)(2,1)}) custom-call(s32[1]{0:T(128)} %bitcast.live_ref, bf16[16,3,16,896]{3,2,1,0:T(8,128)(2,1)} %all-to-all-done.1.rows_ref, bf16[896,4096]{1,0:T(8,128)(2,1)} %w_ref.3, ...), custom_call_target="tpu_custom_call", output_to_operand_aliasing={{0}: (5, {}), {1}: (6, {})} | custom-call | flops 12482248704 | bytes 16777216 | tf_op jit(solution)/shard_map/attend/pallas_call | solution.py:181
  110.1 7.2 %all-to-all-start.4 = ((bf16[32,3,8,896]{3,2,1,0:T(8,128)(2,1)}), bf16[32,3,8,896]{3,2,1,0:T(8,128)(2,1)S(1)}, u32[]{:S(2)}, u32[]{:S(2)}) async-start(bf16[32,3,8,896]{3,2,1,0:T(8,128)(2,1)} %get-tuple-element.22), calls=%async_computation.4 | async-start | bytes 2752512 | tf_op jit(solution)/shard_map/all_to_all | solution.py:246
  117.3 1.5 fusion.5
  118.8 19.0 %all-to-all-done.4 = bf16[32,3,8,896]{3,2,1,0:T(8,128)(2,1)S(1)} async-done(((bf16[32,3,8,896]{3,2,1,0:T(8,128)(2,1)}), bf16[32,3,8,896]{3,2,1,0:T(8,128)(2,1)S(1)}, u32[]{:S(2)}, u32[]{:S(2)}) %all-to-all-start.4) | async-done | bytes 1376288 | tf_op jit(solution)/shard_map/all_to_all | solution.py:246
  137.8 1.8 %fusion = bf16[256,896]{1,0:T(8,128)(2,1)S(1)} fusion(f32[256,896]{1,0:T(8,128)} %fusion.5, bf16[256,768]{1,0:T(8,128)(2,1)S(1)} %get-tuple-element.21, bf16[768,896]{1,0:T(8,128)(2,1)S(1)} %bitcast.19), kind=kOutput, calls=%fused_computation.1 | convolution fusion | flops 352780288 | bytes 3145728 | tf_op jit(solution)/shard_map/dot_general | solution.py:307
  139.6 16.2 %all_to_all.31.pieces_ref = bf16[16,16,896]{2,1,0:T(8,128)(2,1)S(1)} all-to-all(bf16[16,16,896]{2,1,0:T(8,128)(2,1)S(1)} %bitcast.21), channel_id=1, replica_groups=mesh['y'=4,'c'=2,'x'=4,'z'=4] {'x','z'}, dimensions={0} | all-to-all | bytes 917504 | tf_op jit(solution)/shard_map/all_to_all | solution.py:246
  155.8 0.8 collect.1
  (17 shorter events, 0.5 us)
Async XLA Ops:
  21.3 1.9 %collective-permute-start = (bf16[16,15,8,128]{3,2,1,0:T(8,128)(2,1)S(1)}, bf16[16,15,8,128]{3,2,1,0:T(8,128)(2,1)S(1)}, u32[]{:S(2)}, u32[]{:S(2)}) collective-permute-start(bf16[16,15,8,128]{3,2,1,0:T(8,128)(2,1)S(1)} %all_to_all.30.own_ref), channel_id=1, source_target_pairs={{0,16},{16,0},{1,17},{17,1},{2,18},{18,2},{3,19},{19,3},{4,20},{20... | collective-permute-start | bytes 1474568 | tf_op jit(solution)/shard_map/ppermute | solution.py:264
  25.5 26.0 %all-to-all-start.2 = ((bf16[16,3,16,896]{3,2,1,0:T(8,128)(2,1)}), bf16[16,3,16,896]{3,2,1,0:T(8,128)(2,1)S(1)}, u32[]{:S(2)}, u32[]{:S(2)}) async-start(bf16[16,3,16,896]{3,2,1,0:T(8,128)(2,1)} %pack.3), calls=%async_computation.2 | async-start | bytes 2752512 | tf_op jit(solution)/shard_map/all_to_all | solution.py:246
  51.5 27.5 %all-to-all-start.1 = ((bf16[16,3,16,896]{3,2,1,0:T(8,128)(2,1)}), bf16[16,3,16,896]{3,2,1,0:T(8,128)(2,1)}, u32[]{:S(2)}, u32[]{:S(2)}) async-start(bf16[16,3,16,896]{3,2,1,0:T(8,128)(2,1)} %pack.2), calls=%async_computation.1 | async-start | bytes 2752512 | tf_op jit(solution)/shard_map/all_to_all | solution.py:246
  79.0 31.1 %all-to-all-start.3 = ((bf16[32,3,8,896]{3,2,1,0:T(8,128)(2,1)}), bf16[32,3,8,896]{3,2,1,0:T(8,128)(2,1)S(1)}, u32[]{:S(2)}, u32[]{:S(2)}) async-start(bf16[32,3,8,896]{3,2,1,0:T(8,128)(2,1)} %get-tuple-element.20), calls=%async_computation.3 | async-start | bytes 2752512 | tf_op jit(solution)/shard_map/all_to_all | solution.py:246
  110.1 27.7 %all-to-all-start.4 = ((bf16[32,3,8,896]{3,2,1,0:T(8,128)(2,1)}), bf16[32,3,8,896]{3,2,1,0:T(8,128)(2,1)S(1)}, u32[]{:S(2)}, u32[]{:S(2)}) async-start(bf16[32,3,8,896]{3,2,1,0:T(8,128)(2,1)} %get-tuple-element.22), calls=%async_computation.4 | async-start | bytes 2752512 | tf_op jit(solution)/shard_map/all_to_all | solution.py:246

commit v6 on v5

--- a/solution.py
+++ b/solution.py
@@ -16,6 +16,7 @@
 CHUNKS = 2
 HEAD_BATCH = 8
 LANES = 128
+PACK_STEPS = 4
 F32 = jnp.float32
 BF16 = jnp.bfloat16
 
@@ -64,6 +65,8 @@
 def pack_kernel(
     first_group, group_count, chunk_groups, lane_tiles, core_ref, ids_ref, own_ref, other_ref, out_ref
 ):
+    step = pl.program_id(0)
+
     def load(ref_id, t):
         at = (ref_id >> 2, (ref_id & 1) * lane_tiles + t)
         own = ((ref_id >> 1) & 1) == core_ref[0]
@@ -71,7 +74,7 @@
 
     def per_dest(dest, carry):
         for g in range(chunk_groups):
-            at = dest * 2 * group_count + 2 * (first_group + g)
+            at = (step * out_ref.shape[0] + dest) * 2 * group_count + 2 * (first_group + g)
             first, second = ids_ref[at], ids_ref[at + 1]
             for t in range(lane_tiles):
                 a, b = load(first, t), load(second, t)
@@ -94,7 +97,10 @@
             pl.BlockSpec(memory_space=pltpu.VMEM),
             pl.BlockSpec(memory_space=pltpu.VMEM),
         ],
-        out_specs=pl.BlockSpec(memory_space=pltpu.VMEM),
+        grid=(PACK_STEPS,),
+        out_specs=pl.BlockSpec(
+            (dests // PACK_STEPS, chunk_groups, 16, enc), lambda i: (i, 0, 0, 0)
+        ),
         compiler_params=pltpu.CompilerParams(vmem_limit_bytes=16 << 20),
         name="pack",
     )(core, ids, own, other)
@@ -127,7 +133,7 @@
         g_turned[c, in_four] = turned[1][c]
 
     def project(base):
-        rows = rows_ref[:, step].reshape(-1, rows_ref.shape[-1])
+        rows = rows_ref[:, step if first_group == 0 else 0].reshape(-1, rows_ref.shape[-1])
         for start in (base * HD, width + base * HD):
             part = slice(start, start + span)
             kv[:, part] = dot(rows, w_ref[:, part], 1, 0).astype(BF16)
@@ -189,7 +195,9 @@
             num_scalar_prefetch=1,
             grid=(chunk_groups,),
             in_specs=[
-                pl.BlockSpec(memory_space=pltpu.VMEM),
+                pl.BlockSpec(memory_space=pltpu.VMEM)
+                if first_group == 0
+                else pl.BlockSpec((slices, 1, 16, enc), lambda i, l: (0, i, 0, 0)),
                 pl.BlockSpec(weight.shape, lambda i, l: (0, 0), pipeline_mode=pl.Buffered(1)),
                 block,
                 block,

time: 157 us -> 157 us (level)
  no operation moved by 1% of the time
where the time goes in v6:
time: 157 us; the launch traced here: 156 us
  Pallas kernels  53.5 us (34%)
  blocking collectives  47.2 us (30%)
  waiting for transfers between devices  26.9 us (17%)
  starting transfers between devices  23.1 us (15%)
  matrix products  3.26 us (2%)
    pallas_call x2, Pallas kernels, attend(): pl.pallas_call(functools.partial(attend_kernel, width // HD, first_group)...  45.8 us
    all_to_all x2, blocking collectives, exchange(): return lax.all_to_all(block, axes, split_axis=0, concat_axis=0, tiled=True)  35.1 us
    all_to_all x4, waiting for transfers between devices, exchange(): return lax.all_to_all(block, axes, split_axis=0, concat_axis=0, tiled=True)  25.2 us
    all_to_all x4, starting transfers between devices, exchange(): return lax.all_to_all(block, axes, split_axis=0, concat_axis=0, tiled=True)  23.1 us
    all_gather x1, blocking collectives, body(): lax.all_gather(column, DP, axis=0, tiled=False)  12.1 us
    pallas_call x2, Pallas kernels, pack(): pl.pallas_call(functools.partial(pack_kernel, first_group, group_count, c...  5.12 us
    dot_general x2, matrix products, body(): jnp.dot(matches[c], back.reshape(-1, enc), preferred_element_type=F32)  3.26 us
  transfers between devices with their start and end apart: 5, of which 3 were waited for; matrix products, arithmetic and copies ran while one was open for 2% of the time, Pallas kernels for 31%

profile of v6, /device:TPU:0, one launch (start us, length us, event | category | flops | bytes accessed | tf_op | source)
XLA Modules:
  0.0 156.4 jit_solution(5253085129549806630)
XLA Ops:
  0.6 1.8 %spread.1 = bf16[16,15,8,128]{3,2,1,0:T(8,128)(2,1)S(1)} custom-call(s32[1]{0:T(128)} %bitcast.1.core_ref, s32[2,6]{1,0:T(2,128)} %bitcast.25, bf16[4,128,896]{2,1,0:T(8,128)(2,1)} %rows_ref.1), custom_call_target="tpu_custom_call" | custom-call | tf_op jit(solution)/shard_map/spread/pallas_call | solution.py:51
  2.4 18.9 %all_to_all.30.own_ref = bf16[16,15,8,128]{3,2,1,0:T(8,128)(2,1)S(1)} all-to-all(bf16[16,15,8,128]{3,2,1,0:T(8,128)(2,1)S(1)} %spread.1), channel_id=1, replica_groups=mesh['y'=4,'c'=2,'x'=4,'z'=4] {'x','z'}, dimensions={0} | all-to-all | bytes 983040 | tf_op jit(solution)/shard_map/all_to_all | solution.py:254
  21.5 1.6 %collective-permute-done.other_ref = bf16[16,15,8,128]{3,2,1,0:T(8,128)(2,1)S(1)} collective-permute-done((bf16[16,15,8,128]{3,2,1,0:T(8,128)(2,1)S(1)}, bf16[16,15,8,128]{3,2,1,0:T(8,128)(2,1)S(1)}, u32[]{:S(2)}, u32[]{:S(2)}) %collective-permute-start) | collective-permute-done | bytes 491552 | tf_op jit(solution)/shard_map/ppermute | solution.py:272
  23.2 2.6 %pack.3 = bf16[16,3,16,896]{3,2,1,0:T(8,128)(2,1)} custom-call(s32[1]{0:T(128)} %bitcast.1.core_ref, s32[192]{0:T(256)S(1)} %pad_add_fusion.ids_ref, bf16[16,15,8,128]{3,2,1,0:T(8,128)(2,1)S(1)} %all_to_all.30.own_ref, bf16[16,15,8,128]{3,2,1,0:T(8,128)(2,1)S(1)} %collective-permute-done.other_ref), custom_call_target="tpu_custom_call" | custom-call | tf_op jit(solution)/shard_map/pack/pallas_call | solution.py:91
  25.7 3.7 %all-to-all-start.2 = ((bf16[16,3,16,896]{3,2,1,0:T(8,128)(2,1)}), bf16[16,3,16,896]{3,2,1,0:T(8,128)(2,1)S(1)}, u32[]{:S(2)}, u32[]{:S(2)}) async-start(bf16[16,3,16,896]{3,2,1,0:T(8,128)(2,1)} %pack.3), calls=%async_computation.2 | async-start | bytes 2752512 | tf_op jit(solution)/shard_map/all_to_all | solution.py:254
  29.7 2.6 %pack.2 = bf16[16,3,16,896]{3,2,1,0:T(8,128)(2,1)} custom-call(s32[1]{0:T(128)} %bitcast.1.core_ref, s32[192]{0:T(256)S(1)} %pad_add_fusion.ids_ref, bf16[16,15,8,128]{3,2,1,0:T(8,128)(2,1)S(1)} %all_to_all.30.own_ref, bf16[16,15,8,128]{3,2,1,0:T(8,128)(2,1)S(1)} %collective-permute-done.other_ref), custom_call_target="tpu_custom_call" | custom-call | tf_op jit(solution)/shard_map/pack/pallas_call | solution.py:91
  32.2 12.1 %all-gather.1 = s32[8,4,12]{2,1,0:T(4,128)S(1)} all-gather(s32[1,4,12]{2,1,0:T(4,128)S(1)} %bitcast.22), channel_id=2, replica_groups=mesh['y'=4,'c'=2,'x'=4,'z'=4] {'y','c'}, dimensions={0}, use_global_device_ids=true | all-gather | bytes 1728 | tf_op jit(solution)/shard_map/all_gather | solution.py:293
  44.3 0.1 reshape.91
  44.5 0.1 reshape.90
  44.6 0.6 add_select_fusion
  45.2 0.2 eq.31
  45.4 0.2 eq.35
  45.5 6.3 %all-to-all-done.2.rows_ref = bf16[16,3,16,896]{3,2,1,0:T(8,128)(2,1)S(1)} async-done(((bf16[16,3,16,896]{3,2,1,0:T(8,128)(2,1)}), bf16[16,3,16,896]{3,2,1,0:T(8,128)(2,1)S(1)}, u32[]{:S(2)}, u32[]{:S(2)}) %all-to-all-start.2) | async-done | bytes 1376288 | tf_op jit(solution)/shard_map/all_to_all | solution.py:254
  51.8 4.4 %all-to-all-start.1 = ((bf16[16,3,16,896]{3,2,1,0:T(8,128)(2,1)}), bf16[16,3,16,896]{3,2,1,0:T(8,128)(2,1)}, u32[]{:S(2)}, u32[]{:S(2)}) async-start(bf16[16,3,16,896]{3,2,1,0:T(8,128)(2,1)} %pack.2), calls=%async_computation.1 | async-start | bytes 2752512 | tf_op jit(solution)/shard_map/all_to_all | solution.py:254
  56.2 0.2 fusion.1
  56.4 22.9 %attend.2 = (bf16[384,2048]{1,0:T(8,128)(2,1)}, bf16[384,2048]{1,0:T(8,128)(2,1)}, bf16[32,3,8,896]{3,2,1,0:T(8,128)(2,1)}) custom-call(s32[1]{0:T(128)} %bitcast.live_ref, bf16[16,3,16,896]{3,2,1,0:T(8,128)(2,1)S(1)} %all-to-all-done.2.rows_ref, bf16[896,4096]{1,0:T(8,128)(2,1)} %w_ref.3, bf16[384,2048]{1,0:T(8,128)(2,1)} %bitcast.26, ...), custom_call_target="tpu_custom_call" | custom-call | flops 12482248704 | bytes 16777216 | tf_op jit(solution)/shard_map/attend/pallas_call | solution.py:187
  79.3 7.8 %all-to-all-start.3 = ((bf16[32,3,8,896]{3,2,1,0:T(8,128)(2,1)}), bf16[32,3,8,896]{3,2,1,0:T(8,128)(2,1)S(1)}, u32[]{:S(2)}, u32[]{:S(2)}) async-start(bf16[32,3,8,896]{3,2,1,0:T(8,128)(2,1)} %get-tuple-element.20), calls=%async_computation.3 | async-start | bytes 2752512 | tf_op jit(solution)/shard_map/all_to_all | solution.py:254
  87.1 22.9 %attend.3 = (bf16[384,2048]{1,0:T(8,128)(2,1)}, bf16[384,2048]{1,0:T(8,128)(2,1)}, bf16[32,3,8,896]{3,2,1,0:T(8,128)(2,1)}) custom-call(s32[1]{0:T(128)} %bitcast.live_ref, bf16[16,3,16,896]{3,2,1,0:T(8,128)(2,1)} %all-to-all-done.1.rows_ref, bf16[896,4096]{1,0:T(8,128)(2,1)} %w_ref.3, ...), custom_call_target="tpu_custom_call", output_to_operand_aliasing={{0}: (5, {}), {1}: (6, {})} | custom-call | flops 12482248704 | bytes 16777216 | tf_op jit(solution)/shard_map/attend/pallas_call | solution.py:187
  110.0 7.2 %all-to-all-start.4 = ((bf16[32,3,8,896]{3,2,1,0:T(8,128)(2,1)}), bf16[32,3,8,896]{3,2,1,0:T(8,128)(2,1)S(1)}, u32[]{:S(2)}, u32[]{:S(2)}) async-start(bf16[32,3,8,896]{3,2,1,0:T(8,128)(2,1)} %get-tuple-element.22), calls=%async_computation.4 | async-start | bytes 2752512 | tf_op jit(solution)/shard_map/all_to_all | solution.py:254
  117.2 1.5 fusion.5
  118.7 19.0 %all-to-all-done.4 = bf16[32,3,8,896]{3,2,1,0:T(8,128)(2,1)S(1)} async-done(((bf16[32,3,8,896]{3,2,1,0:T(8,128)(2,1)}), bf16[32,3,8,896]{3,2,1,0:T(8,128)(2,1)S(1)}, u32[]{:S(2)}, u32[]{:S(2)}) %all-to-all-start.4) | async-done | bytes 1376288 | tf_op jit(solution)/shard_map/all_to_all | solution.py:254
  137.7 1.8 %fusion = bf16[256,896]{1,0:T(8,128)(2,1)S(1)} fusion(f32[256,896]{1,0:T(8,128)} %fusion.5, bf16[256,768]{1,0:T(8,128)(2,1)S(1)} %get-tuple-element.21, bf16[768,896]{1,0:T(8,128)(2,1)S(1)} %bitcast.19), kind=kOutput, calls=%fused_computation.1 | convolution fusion | flops 352780288 | bytes 3145728 | tf_op jit(solution)/shard_map/dot_general | solution.py:315
  139.5 16.2 %all_to_all.31.pieces_ref = bf16[16,16,896]{2,1,0:T(8,128)(2,1)S(1)} all-to-all(bf16[16,16,896]{2,1,0:T(8,128)(2,1)S(1)} %bitcast.21), channel_id=1, replica_groups=mesh['y'=4,'c'=2,'x'=4,'z'=4] {'x','z'}, dimensions={0} | all-to-all | bytes 917504 | tf_op jit(solution)/shard_map/all_to_all | solution.py:254
  155.7 0.8 collect.1
  (17 shorter events, 0.5 us)
Async XLA Ops:
  21.3 1.9 %collective-permute-start = (bf16[16,15,8,128]{3,2,1,0:T(8,128)(2,1)S(1)}, bf16[16,15,8,128]{3,2,1,0:T(8,128)(2,1)S(1)}, u32[]{:S(2)}, u32[]{:S(2)}) collective-permute-start(bf16[16,15,8,128]{3,2,1,0:T(8,128)(2,1)S(1)} %all_to_all.30.own_ref), channel_id=1, source_target_pairs={{0,16},{16,0},{1,17},{17,1},{2,18},{18,2},{3,19},{19,3},{4,20},{20... | collective-permute-start | bytes 1474568 | tf_op jit(solution)/shard_map/ppermute | solution.py:272
  25.7 26.0 %all-to-all-start.2 = ((bf16[16,3,16,896]{3,2,1,0:T(8,128)(2,1)}), bf16[16,3,16,896]{3,2,1,0:T(8,128)(2,1)S(1)}, u32[]{:S(2)}, u32[]{:S(2)}) async-start(bf16[16,3,16,896]{3,2,1,0:T(8,128)(2,1)} %pack.3), calls=%async_computation.2 | async-start | bytes 2752512 | tf_op jit(solution)/shard_map/all_to_all | solution.py:254
  51.8 27.5 %all-to-all-start.1 = ((bf16[16,3,16,896]{3,2,1,0:T(8,128)(2,1)}), bf16[16,3,16,896]{3,2,1,0:T(8,128)(2,1)}, u32[]{:S(2)}, u32[]{:S(2)}) async-start(bf16[16,3,16,896]{3,2,1,0:T(8,128)(2,1)} %pack.2), calls=%async_computation.1 | async-start | bytes 2752512 | tf_op jit(solution)/shard_map/all_to_all | solution.py:254
  79.3 30.7 %all-to-all-start.3 = ((bf16[32,3,8,896]{3,2,1,0:T(8,128)(2,1)}), bf16[32,3,8,896]{3,2,1,0:T(8,128)(2,1)S(1)}, u32[]{:S(2)}, u32[]{:S(2)}) async-start(bf16[32,3,8,896]{3,2,1,0:T(8,128)(2,1)} %get-tuple-element.20), calls=%async_computation.3 | async-start | bytes 2752512 | tf_op jit(solution)/shard_map/all_to_all | solution.py:254
  110.0 27.7 %all-to-all-start.4 = ((bf16[32,3,8,896]{3,2,1,0:T(8,128)(2,1)}), bf16[32,3,8,896]{3,2,1,0:T(8,128)(2,1)S(1)}, u32[]{:S(2)}, u32[]{:S(2)}) async-start(bf16[32,3,8,896]{3,2,1,0:T(8,128)(2,1)} %get-tuple-element.22), calls=%async_computation.4 | async-start | bytes 2752512 | tf_op jit(solution)/shard_map/all_to_all | solution.py:254
